TPU v7x, 32 devices: a whole 2x2x4 slice. The times are simulated.
32 devices in a mesh: areal: 8 (over y, x, core), layer: 4 (over z).
Axes of the slice: x: 2, y: 2, z: 4, core: 2. Of those that a mesh axis runs over, the one named last changes fastest.
Arguments:
- pressure: float32 [8, 256, 1024], P(None, 'areal', 'layer'), may hold values from 0.7 to 1.4
- composition: float32 [9, 8, 256, 1024], P(None, None, 'areal', 'layer'), may hold values from 0.02 to 1
- mass_old: float32 [9, 8, 256, 1024], P(None, None, 'areal', 'layer'), may hold values from 0 to 0.3
- pore_volume: float32 [8, 256, 1024], P(None, 'areal', 'layer'), may hold values from 0.5 to 2
- trans_x: float32 [8, 256, 1024], P(None, 'areal', 'layer'), may hold values from 0.3 to 3
- trans_y: float32 [8, 256, 1024], P(None, 'areal', 'layer'), may hold values from 0.3 to 3
- trans_z: float32 [8, 256, 1024], P(None, 'areal', 'layer'), may hold values from 0.3 to 3
- volatility: float32 [9], replicated, may hold values from 1.5 to 3
- pressure_slope: float32 [9], replicated, may hold values from 0.2 to 1
- mixing: float32 [9, 9], replicated, may hold values from -3.5 to 3.5
- two_phase: int32 [4, 64], P(None, 'areal'), may hold values from 0 to 1, as said below
Outputs:
- residual: float32 [9, 8, 256, 1024], P(None, None, 'areal', 'layer')
- new_pressure: float32 [8, 256, 1024], P(None, 'areal', 'layer')
Inputs may be any that keep to these rules, and one draw needn't show every extreme that they name: `two_phase`: for each areal index, the 4 rows together flag exactly 16 of their bricks of that areal index, and one of the rows flags all of its 8 bricks of that areal index.
All inputs are finite; a program needn't handle non-finite values.
Results may differ from a plain program's by a relative error of at most 0.0003.
Values sent between devices are 32-bit elements; how exact they have to be, the bound alone decides.
No kernel may reach another device: no remote copies, remote signals or barrier semaphores. Data moves between devices by JAX's collectives and lax.ppermute only.
A program may use at most 128 MiB of HBM per device.

v0:
```python
import functools

import jax
import jax.numpy as jnp
from jax import lax
from jax.experimental import pallas as pl
from jax.experimental.pallas import tpu as pltpu
from jax.sharding import PartitionSpec as P

SS_ITERS = 3
RR_ITERS = 3
LIGHT = 4
COMPS = 9
FIELDS = 16
PRESS, TX, TY, TZ, PORE, MASS = range(COMPS, FIELDS - 1)
H_MOB, H_PRESS, H_TX, H_TY, H_TZ, H_PORE, H_ACC = range(COMPS, FIELDS)
CORNER = (H_MOB, H_PRESS, H_TX, H_TY)
TIME_STEP = 4.0
COMPRESS = 0.2
VAPOUR_WEIGHT = 1.0 / 0.25
LANES = 128
ROWS = 8
MIB = 1024 * 1024
PART = (COMPS + 1) * ROWS
DEEP = 256
PLANES = 4


def rcp(x):
    return pltpu.reciprocal(x, approx=True)


def total_of(terms):
    terms = list(terms)
    while len(terms) > 1:
        terms = [a + b for a, b in zip(terms[::2], terms[1::2])] + (
            [terms[-1]] if len(terms) % 2 else []
        )
    return terms[0]


def split(x):
    high = x.astype(jnp.bfloat16)
    return high, (x - high.astype(jnp.float32)).astype(jnp.bfloat16)


def mixing_operand(mix_ref):
    shape = (ROWS, DEEP)
    lane, row = lane_of(shape), row_of(shape)
    part = lax.div(lane, PART)
    within = lane - PART * part
    column = lax.div(within, ROWS)
    on = (within - ROWS * column == row) & (part < 3)
    blocks = []
    for i in range(COMPS):
        value = jnp.zeros(shape, jnp.float32)
        for j in range(COMPS):
            value = jnp.where(column == j, mix_ref[i, j], value)
        high, low = split(value)
        value = jnp.where(part == 2, low.astype(jnp.float32), high.astype(jnp.float32))
        blocks.append(jnp.where(on, value, 0.0))
    blocks.append(jnp.zeros(shape, jnp.float32))
    return jnp.concatenate(blocks, axis=0).astype(jnp.bfloat16)


def mixed(operand, spread):
    shape = spread[0].shape
    high, low = split(jnp.concatenate(spread + [jnp.zeros(shape, jnp.float32)], axis=0))
    tail = jnp.zeros((DEEP - 3 * PART, shape[1]), jnp.bfloat16)
    out = jnp.dot(
        operand,
        jnp.concatenate([high, low, high, tail], axis=0),
        preferred_element_type=jnp.float32,
    )
    return [out[ROWS * i : ROWS * (i + 1)] for i in range(COMPS)]


def flash(feed, pressure, signed, slope, operand):
    log_press = jnp.log(pressure)
    base = [signed[i] - slope[i] * log_press for i in range(COMPS)]
    spread = None
    for outer in range(SS_ITERS):
        if outer == 0:
            log_k = base
        else:
            mix = mixed(operand, spread)
            log_k = [base[i] - jnp.tanh(mix[i]) for i in range(COMPS)]
        w = [rcp(jnp.exp(log_k[i]) - 1.0) for i in range(COMPS)]
        fraction = jnp.full(pressure.shape, 0.5, jnp.float32)
        for _ in range(RR_ITERS):
            q = [rcp(w[i] + fraction) for i in range(COMPS)]
            part = [feed[i] * q[i] for i in range(COMPS)]
            mismatch = total_of(part)
            gradient = total_of(part[i] * q[i] for i in range(COMPS))
            fraction = jnp.clip(fraction + mismatch * rcp(gradient), 0.0, 1.0)
        spread = [feed[i] * rcp(w[i] + fraction) for i in range(COMPS)]
    liquid_part = (1.0 - fraction) * (1.0 - fraction)
    vapour_part = VAPOUR_WEIGHT * (fraction * fraction)
    both = liquid_part + vapour_part
    return [spread[i] * (both * w[i] + vapour_part) for i in range(COMPS)]


def parameters(vol_ref, slope_ref):
    signed = [vol_ref[i] if i < LIGHT else -vol_ref[i] for i in range(COMPS)]
    return signed, [slope_ref[i] for i in range(COMPS)]


def lane_of(shape):
    return lax.broadcasted_iota(jnp.int32, shape, len(shape) - 1)


def row_of(shape):
    return lax.broadcasted_iota(jnp.int32, shape, len(shape) - 2)


def field_plane(index, z, comp, press, tx, ty, tz, pore, mass):
    if index < COMPS:
        return comp[index, z]
    if index == MASS:
        return total_of(mass[i, z] for i in range(COMPS))
    return {PRESS: press, TX: tx, TY: ty, TZ: tz, PORE: pore}[index][z]


def pack_columns(comp, press, tx, ty, tz, pore, mass, out_ref):
    step = pl.program_id(0)
    planes = press.shape[0]
    shape = (out_ref.shape[0], LANES)
    lane = lane_of(shape)

    @pl.when(step == 0)
    def _():
        out_ref[...] = jnp.zeros(out_ref.shape, jnp.float32)

    for tile in range(FIELDS // 4):
        packed = jnp.zeros(shape, jnp.float32)
        for quarter in range(4):
            index = 4 * tile + quarter
            for z in range(planes if index <= MASS else 0):
                plane = field_plane(index, z, comp, press, tx, ty, tz, pore, mass)
                first, last = plane[:, :LANES], plane[:, -LANES:]
                at = 32 * quarter + 4 * z
                both = jnp.where(lane < LANES // 2, first, last)
                both = pltpu.roll(both, at + 2, 1)
                packed = jnp.where((lane >= at) & (lane < at + 4), both, packed)
        span = pl.ds(tile * LANES, LANES)
        out_ref[:, span] += pltpu.roll(packed, 4 * planes * step, 1)


def own_cells(pack, flags, vol, slope, mix, comp, press, pore, mass, *rest):
    per_tile = 2
    if pack:
        tx, ty, tz, mob_ref, acc_ref, mob_sum, acc_sum, low_ref, high_ref, operand = rest
        tile_row = pl.program_id(0) * (flags.shape[1] // per_tile - 1)
    else:
        mob_ref, acc_ref, mob_sum, acc_sum, operand = rest[-5:]
        tile_row = pl.program_id(0) + 1
    layer = lax.axis_index("layer")
    signed, slopes = parameters(vol, slope)
    planes, _, width = press.shape

    @pl.when((pl.program_id(0) == 0) & (pl.program_id(1) == 0))
    def _():
        operand[...] = mixing_operand(mix)

    raw = [comp[i] for i in range(COMPS)]
    inverse = rcp(total_of(raw))
    feed = [raw[i] * inverse for i in range(COMPS)]
    volume = pore[...]
    acc = [volume * feed[i] - mass[i] for i in range(COMPS)]
    for i in range(COMPS):
        acc_ref[i] = acc[i]
    acc_sum[...] = total_of(acc)
    tile_flags = [flags[layer, tile_row * per_tile + b] for b in range(per_tile)]
    some = tile_flags[0] + tile_flags[1]

    @pl.when(some > 0)
    def _():
        def beside(x):
            return jnp.concatenate([x[z] for z in range(planes)], axis=1)

        here = [beside(feed[i]) for i in range(COMPS)]
        two = flash(here, beside(press), signed, slopes, operand[...])
        marked = jnp.where(row_of(here[0].shape) < ROWS // per_tile, tile_flags[0], tile_flags[1])
        mobility = [jnp.where(marked > 0, two[i], here[i]) for i in range(COMPS)]
        total = total_of(mobility)
        for z in range(planes):
            span = slice(z * width, (z + 1) * width)
            for i in range(COMPS):
                mob_ref[i, z] = mobility[i][:, span]
            mob_sum[z] = total[:, span]

    @pl.when(some == 0)
    def _():
        for i in range(COMPS):
            mob_ref[i] = feed[i]
        mob_sum[...] = total_of(feed)

    if not pack:
        return
    rest_fields = {
        H_MOB: mob_sum, H_PRESS: press, H_TX: tx, H_TY: ty, H_TZ: tz, H_PORE: pore, H_ACC: acc_sum,
    }

    def field(k, z):
        return mob_ref[k, z] if k < COMPS else rest_fields[k][z]

    half = FIELDS // 2
    row = row_of((ROWS, width))

    @pl.when(pl.program_id(0) == 0)
    def _():
        for k in range(half):
            for pair in range(planes // 2):
                near, far = [
                    jnp.where(row % 4 >= 2, pltpu.roll(field(k, z), 2, 0), field(k + half, z))
                    for z in (2 * pair, 2 * pair + 1)
                ]
                low_ref[k, pl.ds(pair * ROWS, ROWS), :] = jnp.where(row < 4, near, pltpu.roll(far, 4, 0))

    @pl.when(pl.program_id(0) == 1)
    def _():
        for k in range(half):
            for pair in range(planes // 2):
                near, far = [
                    jnp.where(
                        row % 4 < 2, pltpu.roll(field(k, z), 2, 0), pltpu.roll(field(k + half, z), 4, 0)
                    )
                    for z in (2 * pair, 2 * pair + 1)
                ]
                high_ref[k, pl.ds(pair * ROWS, ROWS), :] = jnp.where(row < 4, near, pltpu.roll(far, 4, 0))


def column_cells(flags, vol, slope, mix, left, right, low_in, high_in, out_ref, low_ref, high_ref):
    del low_in, high_in
    rows = left.shape[0]
    shape = (rows, LANES)
    lane = lane_of(shape)
    raw = []
    for tile in range(FIELDS // 4):
        span = slice(tile * LANES, (tile + 1) * LANES)
        columns = jnp.where(lane % 4 < 2, left[:, span], right[:, span])
        for quarter in range(4):
            turn = (LANES - 32 * quarter) % LANES
            raw.append(pltpu.roll(columns, turn, 1) if turn else columns)
    total = total_of(raw[:COMPS])
    there = (total > 0.0) & (lane < 32)
    inverse = rcp(jnp.where(there, total, 1.0))
    feed = [jnp.where(there, raw[i] * inverse, 1.0) for i in range(COMPS)]
    signed, slopes = parameters(vol, slope)
    layer, layers = lax.axis_index("layer"), lax.axis_size("layer")
    bricks = flags.shape[1]
    brick = lax.div(row_of(shape), rows // bricks)
    marked = jnp.zeros(shape, jnp.int32)
    for b in range(bricks):
        both = jnp.where(
            lane % 4 < 2, flags[jnp.maximum(layer - 1, 0), b], flags[jnp.minimum(layer + 1, layers - 1), b]
        )
        marked = jnp.where(brick == b, both, marked)

    def beside(x):
        return jnp.concatenate([x[t : t + ROWS] for t in range(0, rows, ROWS)], axis=1)

    def above(x):
        return jnp.concatenate([x[:, t : t + LANES] for t in range(0, x.shape[1], LANES)], axis=0)

    pressure = jnp.where(there, raw[PRESS], 1.0)
    two = flash([beside(x) for x in feed], beside(pressure), signed, slopes, mixing_operand(mix))
    mobility = [
        jnp.where(there, jnp.where(marked > 0, above(two[i]), feed[i]), 0.0) for i in range(COMPS)
    ]
    fields = mobility + [total_of(mobility), raw[PRESS], raw[TX], raw[TY], raw[TZ], raw[PORE]]
    fields.append(raw[PORE] - raw[MASS])
    for k in range(FIELDS):
        out_ref[k] = fields[k]
    corner = fields[CORNER[0]]
    for quarter in range(1, 4):
        at = 32 * quarter
        corner = jnp.where(
            (lane >= at) & (lane < at + 32), pltpu.roll(fields[CORNER[quarter]], at, 1), corner
        )
    low_ref[0] = corner[:ROWS]
    high_ref[0] = corner[rows - ROWS :]


def finish(
    columns, above, below,
    press, tx, ty, tz, pore, mob_sum, acc_sum, mob, acc,
    res_ref, new_ref,
    rows_h, columns_h, e_press, e_tx, e_ty, e_tz, e_pore, e_mob, e_acc,
    g_x, g_y, g_z, c_x, c_y, c_z, first,
):
    step = pl.program_id(0)
    planes = res_ref.shape[1]
    depth, rows, width = press.shape
    layer, layers = lax.axis_index("layer"), lax.axis_size("layer")
    areal, areals = lax.axis_index("areal"), lax.axis_size("areal")
    half = FIELDS // 2
    tall, wide = rows + ROWS, width + LANES
    full = (tall, wide)
    own = (slice(0, rows), slice(0, width))
    extended = {
        H_MOB: (e_mob, mob_sum), H_PRESS: (e_press, press), H_TX: (e_tx, tx), H_TY: (e_ty, ty),
        H_TZ: (e_tz, tz), H_PORE: (e_pore, pore), H_ACC: (e_acc, acc_sum),
    }

    @pl.when(step == 0)
    def _():
        upper = row_of((rows, width)) % 4 < 2
        corner_row = row_of((ROWS, LANES))
        corners = jnp.where(corner_row < 4, below[half, 0:ROWS, 0:LANES], above[half, 0:ROWS, 0:LANES])
        for k in range(FIELDS):
            up, down = above[k % half], below[k % half]
            if k < half:
                beside = jnp.where(upper, up, down)
            else:
                beside = jnp.where(upper, pltpu.roll(up, rows - 2, 0), pltpu.roll(down, 2, 0))
            column = columns[k]
            for z in range(depth):
                at = (z // 2) * ROWS
                tile = pltpu.roll(beside[at : at + ROWS], 6 - 4 * (z % 2), 0)
                turn = (LANES + LANES - 2 - 4 * z) % LANES
                side = pltpu.roll(column, turn, 1)
                if k < COMPS:
                    rows_h[k, z] = tile
                    columns_h[k, z] = side
                else:
                    e_ref, own_ref = extended[k]
                    e_ref[z, pl.ds(0, rows), pl.ds(0, width)] = own_ref[z]
                    e_ref[z, pl.ds(rows, ROWS), pl.ds(0, width)] = tile
                    e_ref[z, pl.ds(0, rows), pl.ds(width, LANES)] = side
                    if k in CORNER:
                        turn = (turn + LANES - 32 * CORNER.index(k)) % LANES
                        e_ref[z, pl.ds(rows, ROWS), pl.ds(width, LANES)] = pltpu.roll(corners, turn, 1)

        end_x = (row_of(full) == rows - 1) & (areal == areals - 1)
        end_y = (lane_of(full) == width - 1) & (layer == layers - 1)
        scale = 0.5 * TIME_STEP
        nothing = jnp.zeros(full, jnp.float32)
        g_z[0] = nothing
        c_z[0] = nothing

        def update(z):
            p, m = e_press[z], e_mob[z]
            up, down = jnp.minimum(z + 1, depth - 1), jnp.maximum(z - 1, 0)
            strength_x = jnp.where(end_x, 0.0, scale * e_tx[z])
            strength_y = jnp.where(end_y, 0.0, scale * e_ty[z])
            strength_z = jnp.where(z < depth - 1, scale, 0.0) * e_tz[z]
            dx = p - pltpu.roll(p, tall - 1, 0)
            dy = p - pltpu.roll(p, wide - 1, 1)
            dz = p - e_press[up]
            cx = strength_x * (m + pltpu.roll(m, tall - 1, 0))
            cy = strength_y * (m + pltpu.roll(m, wide - 1, 1))
            cz = strength_z * (m + e_mob[up])
            cz_low = c_z[z]
            g_x[z], g_y[z], g_z[z + 1] = strength_x * dx, strength_y * dy, strength_z * dz
            c_x[z], c_y[z], c_z[z + 1] = cx, cy, cz
            fx, fy = cx * dx, cy * dy
            total = (
                e_acc[z]
                + (fx - pltpu.roll(fx, 1, 0))
                + (fy - pltpu.roll(fy, 1, 1))
                + (cz * dz + cz_low * (p - e_press[down]))
            )
            diagonal = (
                COMPRESS * e_pore[z]
                + (cx + pltpu.roll(cx, 1, 0))
                + (cy + pltpu.roll(cy, 1, 1))
                + (cz + cz_low)
            )
            inverse = rcp(jnp.where(diagonal > 0.0, diagonal, 1.0))
            first[z] = jnp.where(diagonal > 0.0, -total * inverse, 0.0)
            e_acc[z] = total
            e_pore[z] = inverse

        def second(z):
            here = first[z]
            up, down = jnp.minimum(z + 1, depth - 1), jnp.maximum(z - 1, 0)
            cx, cy = c_x[z], c_y[z]
            near = (
                (cx * pltpu.roll(here, tall - 1, 0))[own]
                + pltpu.roll(cx * here, 1, 0)[own]
                + (cy * pltpu.roll(here, wide - 1, 1))[own]
                + pltpu.roll(cy * here, 1, 1)[own]
                + (c_z[z + 1] * first[up] + c_z[z] * first[down])[own]
                - e_acc[z][own]
            )
            new_ref[z] = e_press[z][own] + near * e_pore[z][own]

        for body in (update, second):
            def pair(t, carry):
                body(2 * t)
                body(2 * t + 1)
                return carry

            lax.fori_loop(0, depth // 2, pair, 0)

    for plane in range(planes):
        z = step * planes + plane
        down, up = jnp.maximum(z - 1, 0), jnp.minimum(z + 1, depth - 1)
        gx, gy = g_x[z], g_y[z]
        gx_low = -pltpu.roll(gx, 1, 0)[own]
        gy_low = -pltpu.roll(gy, 1, 1)[own]
        gz, gz_low = g_z[z + 1][own], -g_z[z][own]
        gx, gy = gx[own], gy[own]
        middle = (gx + gx_low) + (gy + gy_low) + (gz + gz_low)
        for i in range(COMPS):
            here = mob[i, z]
            tall_here = jnp.concatenate([here, rows_h[i, z]], axis=0)
            wide_here = jnp.concatenate([here, columns_h[i, z]], axis=1)
            res_ref[i, plane] = (
                acc[i, z]
                + middle * here
                + gx * pltpu.roll(tall_here, tall - 1, 0)[own]
                + gx_low * pltpu.roll(tall_here, 1, 0)[own]
                + gy * pltpu.roll(wide_here, wide - 1, 1)[own]
                + gy_low * pltpu.roll(wide_here, 1, 1)[own]
                + gz * mob[i, up]
                + gz_low * mob[i, down]
            )


def on_device(
    pressure, composition, mass_old, pore_volume, trans_x, trans_y, trans_z,
    volatility, pressure_slope, mixing, two_phase,
):
    depth, rows, width = pressure.shape
    f32 = jnp.float32
    smem = pl.BlockSpec(memory_space=pltpu.SMEM)
    vmem = pl.BlockSpec(memory_space=pltpu.VMEM)
    half = FIELDS // 2

    def params(mib):
        return pltpu.CompilerParams(vmem_limit_bytes=mib * MIB)

    scalars = (two_phase, volatility, pressure_slope, mixing)

    def moved(block, axis, shift):
        count = lax.axis_size(axis)
        pairs = [(i, i + shift) for i in range(count) if 0 <= i + shift < count]
        return lax.ppermute(block, axis, pairs)

    fields = (composition, pressure, trans_x, trans_y, trans_z, pore_volume, mass_old)
    plane = pl.BlockSpec((PLANES, rows, width), lambda s: (s, 0, 0))
    planes = pl.BlockSpec((COMPS, PLANES, rows, width), lambda s: (0, s, 0, 0))
    packet = pl.pallas_call(
        pack_columns,
        grid=(depth // PLANES,),
        in_specs=[planes, plane, plane, plane, plane, plane, planes],
        out_specs=vmem,
        out_shape=jax.ShapeDtypeStruct((rows, FIELDS * 32), f32),
        compiler_params=params(24),
        name="pack_columns",
    )(*[pltpu.with_memory_space_constraint(field, pltpu.HBM) for field in fields])
    left = moved(packet, "layer", 1)
    right = moved(packet, "layer", -1)

    whole = jax.ShapeDtypeStruct((COMPS, depth, rows, width), f32)
    sums = jax.ShapeDtypeStruct((depth, rows, width), f32)
    packed = jax.ShapeDtypeStruct((half + 1, 4 * depth, width), f32)
    parts = depth // PLANES
    tiles = rows // ROWS

    def own(pack, before):
        tile_row = (lambda g: g * (tiles - 1)) if pack else (lambda g: g + 1)
        plane = pl.BlockSpec((PLANES, ROWS, width), lambda g, z: (z, tile_row(g), 0))
        planes = pl.BlockSpec((COMPS, PLANES, ROWS, width), lambda g, z: (0, z, tile_row(g), 0))
        block = (half, 4 * PLANES, width)
        low = pl.BlockSpec(block, lambda g, z: (0, jnp.where(g == 0, z, parts - 1), 0))
        high = pl.BlockSpec(block, lambda g, z: (0, jnp.where(g == 0, 0, z), 0))
        count = 2 if pack else tiles - 2
        cells = count * ROWS * depth * width
        return pl.pallas_call(
            functools.partial(own_cells, pack),
            grid=(count, parts),
            in_specs=[smem] * 4
            + [planes, plane, plane, planes]
            + [plane] * (3 if pack else 0)
            + [pl.BlockSpec(memory_space=pl.ANY)] * len(before),
            out_specs=[planes, planes, plane, plane] + ([low, high] if pack else []),
            out_shape=[whole, whole, sums, sums] + ([packed, packed] if pack else []),
            input_output_aliases={8 + k: k for k in range(len(before))},
            scratch_shapes=[pltpu.VMEM((PART, DEEP), jnp.bfloat16)],
            compiler_params=params(24),
            cost_estimate=pl.CostEstimate(
                flops=900 * cells, transcendentals=190 * cells, bytes_accessed=4 * 39 * cells
            ),
            name="edge_cells" if pack else "inner_cells",
        )(
            *scalars, composition, pressure, pore_volume, mass_old,
            *((trans_x, trans_y, trans_z) if pack else ()), *before,
        )

    *begun, low, high = own(True, ())

    left, right, low, high, begun = lax.optimization_barrier((left, right, low, high, begun))
    corner = pl.BlockSpec((1, ROWS, LANES), lambda s: (half, 0, 0))
    columns, low, high = pl.pallas_call(
        column_cells,
        grid=(1,),
        in_specs=[smem] * 4 + [vmem] * 2 + [pl.BlockSpec(memory_space=pl.ANY)] * 2,
        out_specs=[vmem, corner, corner],
        out_shape=[jax.ShapeDtypeStruct((FIELDS, rows, LANES), f32), packed, packed],
        input_output_aliases={6: 1, 7: 2},
        compiler_params=params(16),
        name="column_cells",
    )(*scalars, left, right, low, high)
    above = moved(high, "areal", 1)
    below = moved(low, "areal", -1)

    mob, acc, mob_sum, acc_sum = own(False, begun)

    planes = pl.BlockSpec((COMPS, 2, rows, width), lambda s: (0, s, 0, 0))
    extended = pltpu.VMEM((depth, rows + ROWS, width + LANES), f32)
    above_faces = pltpu.VMEM((depth + 1, rows + ROWS, width + LANES), f32)
    return pl.pallas_call(
        finish,
        grid=(depth // 2,),
        in_specs=[vmem] * 12,
        out_specs=[planes, vmem],
        out_shape=[whole, sums],
        scratch_shapes=[
            pltpu.VMEM((COMPS, depth, ROWS, width), f32),
            pltpu.VMEM((COMPS, depth, rows, LANES), f32),
            *[extended] * 7,
            *[extended, extended, above_faces] * 2,
            extended,
        ],
        compiler_params=params(28),
        name="finish",
    )(
        columns, above, below,
        pressure, trans_x, trans_y, trans_z, pore_volume, mob_sum, acc_sum, mob, acc,
    )


def solution(mesh):
    placed = (
        P(None, "areal", "layer"),
        P(None, None, "areal", "layer"),
        P(None, None, "areal", "layer"),
        P(None, "areal", "layer"),
        P(None, "areal", "layer"),
        P(None, "areal", "layer"),
        P(None, "areal", "layer"),
        P(),
        P(),
        P(),
        P(None, "areal"),
    )
    return jax.shard_map(
        on_device,
        mesh=mesh,
        in_specs=placed,
        out_specs=(P(None, None, "areal", "layer"), P(None, "areal", "layer")),
        check_vma=False,
    )
```

profile of v0, /device:TPU:12, one launch (start us, length us, event | category | flops | bytes accessed | tf_op | source)
XLA Modules:
  0.0 39.1 jit_solution(3394080511052682205)
XLA Ops:
  0.6 0.0 copy-start.2
  0.6 0.0 copy-start
  0.7 0.0 copy-start.1
  0.7 0.0 copy-start.6
  0.7 0.0 copy-start.3
  0.7 0.0 copy-start.4
  0.7 0.0 copy-start.5
  0.7 0.0 copy-start.9
  0.7 0.0 copy-start.10
  0.7 0.0 copy-start.7
  0.7 0.0 copy-start.8
  0.7 3.4 %pack_columns.1 = f32[32,512]{1,0:T(8,128)S(1)} custom-call(f32[9,8,32,256]{3,2,1,0:T(8,128)} %comp.5, f32[8,32,256]{2,1,0:T(8,128)} %press.7, f32[8,32,256]{2,1,0:T(8,128)} %tx.3, f32[8,32,256]{2,1,0:T(8,128)} %ty.3, f32[8,32,256]{2,1,0:T(8,128)} %tz.3, f32[8,32,256]{2,1,0:T(8,128)} %pore.7, f32[9,8,32,256]{3,2,1,0:T(8,128)} %mass.5), custom_call_target="tpu_custom_call" | custom-call | tf_op jit(solution)/shard_map/pack_columns/pallas_call | solution.py:445
  4.2 3.6 %collective-permute-start = (f32[32,512]{1,0:T(8,128)S(1)}, f32[32,512]{1,0:T(8,128)S(1)}, u32[]{:S(2)}, u32[]{:S(2)}) collective-permute-start(f32[32,512]{1,0:T(8,128)S(1)} %pack_columns.1), channel_id=1, source_target_pairs={{0,1},{1,2},{2,3},{4,5},{5,6},{6,7},{8,9},{9,10},{10,11},{12,13},{... | collective-permute-start | bytes 196616 | tf_op jit(solution)/shard_map/ppermute | solution.py:440
  7.8 2.4 %collective-permute-start.1 = (f32[32,512]{1,0:T(8,128)S(1)}, f32[32,512]{1,0:T(8,128)S(1)}, u32[]{:S(2)}, u32[]{:S(2)}) collective-permute-start(f32[32,512]{1,0:T(8,128)S(1)} %pack_columns.1), channel_id=1, source_target_pairs={{1,0},{2,1},{3,2},{5,4},{6,5},{7,6},{9,8},{10,9},{11,10},{13,12},{... | collective-permute-start | bytes 196616 | tf_op jit(solution)/shard_map/ppermute | solution.py:440
  10.2 0.0 copy-done.2
  10.2 0.0 copy-done
  10.2 0.0 copy-done.1
  10.2 0.0 copy-done.6
  10.2 0.0 copy-done.3
  10.2 0.0 copy-done.4
  10.2 0.0 copy-done.5
  10.2 0.0 copy-done.9
  10.3 7.3 %edge_cells.1 = (f32[9,8,32,256]{3,2,1,0:T(8,128)S(1)}, f32[9,8,32,256]{3,2,1,0:T(8,128)S(1)}, f32[8,32,256]{2,1,0:T(8,128)S(1)}, f32[8,32,256]{2,1,0:T(8,128)S(...) custom-call(s32[4,8]{1,0:T(4,128)S(1)} %copy-done.8, f32[9]{0:T(128)S(1)} %copy-done.9, f32[9]{0:T(128)S(1)} %copy-done.10, ...), custom_call_target="tpu_custom_call" | custom-call | flops 29491200 | bytes 5111808 | tf_op jit(solution)/shard_map/edge_cells/pallas_call | solution.py:472
  17.6 0.0 collective-permute-done.left
  17.6 0.0 collective-permute-done.1.right
  17.6 1.7 %column_cells.1 = (f32[16,32,128]{2,1,0:T(8,128)S(1)}, f32[9,32,256]{2,1,0:T(8,128)S(1)}, f32[9,32,256]{2,1,0:T(8,128)S(1)}) custom-call(s32[4,8]{1,0:T(4,128)S(1)} %copy-done.8, f32[9]{0:T(128)S(1)} %copy-done.9, f32[9]{0:T(128)S(1)} %copy-done.10, f32[9,9]{1,0:T(8,128)S(1)} %copy-done.7, ...), custom_call_target="tpu_custom_call", output_to_operand_aliasing={{1}: (6, {}), {2}: (7, {})} | custom-call | tf_op jit(solution)/shard_map/column_cells/pallas_call | solution.py:497
  19.4 1.9 %collective-permute-start.2 = (f32[9,32,256]{2,1,0:T(8,128)S(1)}, f32[9,32,256]{2,1,0:T(8,128)S(1)}, u32[]{:S(2)}, u32[]{:S(2)}) collective-permute-start(f32[9,32,256]{2,1,0:T(8,128)S(1)} %get-tuple-element.34), channel_id=1, source_target_pairs={{0,4},{4,8},{8,12},{12,16},{16,20},{20,24},{24,28},{1,5},{5,9},{9,... | collective-permute-start | bytes 884744 | tf_op jit(solution)/shard_map/ppermute | solution.py:440
  21.3 4.5 %collective-permute-start.3 = (f32[9,32,256]{2,1,0:T(8,128)S(1)}, f32[9,32,256]{2,1,0:T(8,128)S(1)}, u32[]{:S(2)}, u32[]{:S(2)}) collective-permute-start(f32[9,32,256]{2,1,0:T(8,128)S(1)} %get-tuple-element.35), channel_id=1, source_target_pairs={{4,0},{8,4},{12,8},{16,12},{20,16},{24,20},{28,24},{5,1},{9,5},{13... | collective-permute-start | bytes 884744 | tf_op jit(solution)/shard_map/ppermute | solution.py:440
  25.8 6.9 %inner_cells.1 = (f32[9,8,32,256]{3,2,1,0:T(8,128)S(1)}, f32[9,8,32,256]{3,2,1,0:T(8,128)S(1)}, f32[8,32,256]{2,1,0:T(8,128)S(1)}, f32[8,32,256]{2,1,0:T(8,128)S(1)}) custom-call(s32[4,8]{1,0:T(4,128)S(1)} %copy-done.8, f32[9]{0:T(128)S(1)} %copy-done.9, f32[9]{0:T(128)S(1)} %copy-done.10, ...), custom_call_target="tpu_custom_call", output_to_operand_aliasing={{0}: (8, {}), {1}: (9, {}), {2}: (10, {}), {3}: (11, {})} | custom-call | flops 29491200 | bytes 5111808 | tf_op jit(solution)/shard_map/inner_cells/pallas_call | solution.py:472
  32.8 0.0 collective-permute-done.2.above
  32.8 0.0 collective-permute-done.3.below
  32.8 6.3 %finish.1 = (f32[9,8,32,256]{3,2,1,0:T(8,128)}, f32[8,32,256]{2,1,0:T(8,128)}) custom-call(f32[16,32,128]{2,1,0:T(8,128)S(1)} %get-tuple-element.33.columns, f32[9,32,256]{2,1,0:T(8,128)S(1)} %collective-permute-done.2.above, f32[9,32,256]{2,1,0:T(8,128)S(1)} %collective-permute-done.3.below, f32[8,32,256]{2,1,0:T(8,128)S(1)} %copy-done.2, ...), custom_call_target="tpu_custom_call" | custom-call | tf_op jit(solution)/shard_map/finish/pallas_call | solution.py:515
  (3 shorter events, 0.0 us)
Async XLA Ops:
  0.6 9.5 %copy-start.2 = (f32[8,32,256]{2,1,0:T(8,128)S(1)}, f32[8,32,256]{2,1,0:T(8,128)}, u32[]{:S(2)}) copy-start(f32[8,32,256]{2,1,0:T(8,128)} %press.7) | copy-start | bytes 786436
  0.6 9.5 %copy-start = (f32[9,8,32,256]{3,2,1,0:T(8,128)S(1)}, f32[9,8,32,256]{3,2,1,0:T(8,128)}, u32[]{:S(2)}) copy-start(f32[9,8,32,256]{3,2,1,0:T(8,128)} %comp.5) | copy-start | bytes 7077892
  0.7 9.5 %copy-start.1 = (f32[9,8,32,256]{3,2,1,0:T(8,128)S(1)}, f32[9,8,32,256]{3,2,1,0:T(8,128)}, u32[]{:S(2)}) copy-start(f32[9,8,32,256]{3,2,1,0:T(8,128)} %mass.5) | copy-start | bytes 7077892
  0.7 9.5 %copy-start.6 = (f32[8,32,256]{2,1,0:T(8,128)S(1)}, f32[8,32,256]{2,1,0:T(8,128)}, u32[]{:S(2)}) copy-start(f32[8,32,256]{2,1,0:T(8,128)} %pore.7) | copy-start | bytes 786436
  0.7 9.5 %copy-start.3 = (f32[8,32,256]{2,1,0:T(8,128)S(1)}, f32[8,32,256]{2,1,0:T(8,128)}, u32[]{:S(2)}) copy-start(f32[8,32,256]{2,1,0:T(8,128)} %tx.3) | copy-start | bytes 786436
  0.7 9.5 %copy-start.4 = (f32[8,32,256]{2,1,0:T(8,128)S(1)}, f32[8,32,256]{2,1,0:T(8,128)}, u32[]{:S(2)}) copy-start(f32[8,32,256]{2,1,0:T(8,128)} %ty.3) | copy-start | bytes 786436
  0.7 9.5 %copy-start.5 = (f32[8,32,256]{2,1,0:T(8,128)S(1)}, f32[8,32,256]{2,1,0:T(8,128)}, u32[]{:S(2)}) copy-start(f32[8,32,256]{2,1,0:T(8,128)} %tz.3) | copy-start | bytes 786436
  0.7 9.5 %copy-start.9 = (f32[9]{0:T(128)S(1)}, f32[9]{0:T(128)}, u32[]{:S(2)}) copy-start(f32[9]{0:T(128)} %vol.5) | copy-start | bytes 112
  0.7 9.5 %copy-start.10 = (f32[9]{0:T(128)S(1)}, f32[9]{0:T(128)}, u32[]{:S(2)}) copy-start(f32[9]{0:T(128)} %slope.5) | copy-start | bytes 112
  0.7 9.5 %copy-start.7 = (f32[9,9]{1,0:T(8,128)S(1)}, f32[9,9]{1,0:T(8,128)}, u32[]{:S(2)}) copy-start(f32[9,9]{1,0:T(8,128)} %mix.5) | copy-start | bytes 976
  0.7 9.5 %copy-start.8 = (s32[4,8]{1,0:T(4,128)S(1)}, s32[4,8]{1,0:T(4,128)}, u32[]{:S(2)}) copy-start(s32[4,8]{1,0:T(4,128)} %flags.5) | copy-start | bytes 388
  4.2 13.4 %collective-permute-start = (f32[32,512]{1,0:T(8,128)S(1)}, f32[32,512]{1,0:T(8,128)S(1)}, u32[]{:S(2)}, u32[]{:S(2)}) collective-permute-start(f32[32,512]{1,0:T(8,128)S(1)} %pack_columns.1), channel_id=1, source_target_pairs={{0,1},{1,2},{2,3},{4,5},{5,6},{6,7},{8,9},{9,10},{10,11},{12,13},{... | collective-permute-start | bytes 196616 | tf_op jit(solution)/shard_map/ppermute | solution.py:440
  7.8 9.8 %collective-permute-start.1 = (f32[32,512]{1,0:T(8,128)S(1)}, f32[32,512]{1,0:T(8,128)S(1)}, u32[]{:S(2)}, u32[]{:S(2)}) collective-permute-start(f32[32,512]{1,0:T(8,128)S(1)} %pack_columns.1), channel_id=1, source_target_pairs={{1,0},{2,1},{3,2},{5,4},{6,5},{7,6},{9,8},{10,9},{11,10},{13,12},{... | collective-permute-start | bytes 196616 | tf_op jit(solution)/shard_map/ppermute | solution.py:440
  19.4 13.4 %collective-permute-start.2 = (f32[9,32,256]{2,1,0:T(8,128)S(1)}, f32[9,32,256]{2,1,0:T(8,128)S(1)}, u32[]{:S(2)}, u32[]{:S(2)}) collective-permute-start(f32[9,32,256]{2,1,0:T(8,128)S(1)} %get-tuple-element.34), channel_id=1, source_target_pairs={{0,4},{4,8},{8,12},{12,16},{16,20},{20,24},{24,28},{1,5},{5,9},{9,... | collective-permute-start | bytes 884744 | tf_op jit(solution)/shard_map/ppermute | solution.py:440
  21.3 11.5 %collective-permute-start.3 = (f32[9,32,256]{2,1,0:T(8,128)S(1)}, f32[9,32,256]{2,1,0:T(8,128)S(1)}, u32[]{:S(2)}, u32[]{:S(2)}) collective-permute-start(f32[9,32,256]{2,1,0:T(8,128)S(1)} %get-tuple-element.35), channel_id=1, source_target_pairs={{4,0},{8,4},{12,8},{16,12},{20,16},{24,20},{28,24},{5,1},{9,5},{13... | collective-permute-start | bytes 884744 | tf_op jit(solution)/shard_map/ppermute | solution.py:440
where the time goes:
time: 39.3 us; the launch traced here: 39.1 us
  Pallas kernels  25.7 us (65%)
  starting transfers between devices  12.4 us (32%)
  between operations  0.9 us (2%)
    pallas_call x2, Pallas kernels, own(): pl.pallas_call(functools.partial(own_cells, pack), grid=(count, parts), i...  14.2 us
    ppermute x4, starting transfers between devices, moved(): return lax.ppermute(block, axis, pairs)  12.4 us
    pallas_call x1, Pallas kernels, on_device(): pl.pallas_call(finish, grid=(depth // 2,), in_specs=[vmem] * 12, out_spec...  6.31 us
    pallas_call x1, Pallas kernels, on_device(): pl.pallas_call(pack_columns, grid=(depth // PLANES,), in_specs=[planes, p...  3.44 us
    pallas_call x1, Pallas kernels, on_device(): pl.pallas_call(column_cells, grid=(1,), in_specs=[smem] * 4 + [vmem] * 2...  1.72 us
  transfers between devices with their start and end apart: 4, of which 0 were waited for; matrix products, arithmetic and copies ran while one was open for 0% of the time, Pallas kernels for 36%

commit v1 on v0

--- a/solution.py
+++ b/solution.py
@@ -39,6 +39,16 @@
     return terms[0]
 
 
+def inverses(values):
+    out = []
+    for a, b in zip(values[::2], values[1::2]):
+        both = rcp(a * b)
+        out += [b * both, a * both]
+    if len(values) % 2:
+        out.append(rcp(values[-1]))
+    return out
+
+
 def split(x):
     high = x.astype(jnp.bfloat16)
     return high, (x - high.astype(jnp.float32)).astype(jnp.bfloat16)
@@ -85,15 +95,16 @@
         else:
             mix = mixed(operand, spread)
             log_k = [base[i] - jnp.tanh(mix[i]) for i in range(COMPS)]
-        w = [rcp(jnp.exp(log_k[i]) - 1.0) for i in range(COMPS)]
+        w = inverses([jnp.exp(log_k[i]) - 1.0 for i in range(COMPS)])
         fraction = jnp.full(pressure.shape, 0.5, jnp.float32)
         for _ in range(RR_ITERS):
-            q = [rcp(w[i] + fraction) for i in range(COMPS)]
+            q = inverses([w[i] + fraction for i in range(COMPS)])
             part = [feed[i] * q[i] for i in range(COMPS)]
             mismatch = total_of(part)
             gradient = total_of(part[i] * q[i] for i in range(COMPS))
             fraction = jnp.clip(fraction + mismatch * rcp(gradient), 0.0, 1.0)
-        spread = [feed[i] * rcp(w[i] + fraction) for i in range(COMPS)]
+        q = inverses([w[i] + fraction for i in range(COMPS)])
+        spread = [feed[i] * q[i] for i in range(COMPS)]
     liquid_part = (1.0 - fraction) * (1.0 - fraction)
     vapour_part = VAPOUR_WEIGHT * (fraction * fraction)
     both = liquid_part + vapour_part
@@ -121,9 +132,8 @@
     return {PRESS: press, TX: tx, TY: ty, TZ: tz, PORE: pore}[index][z]
 
 
-def pack_columns(comp, press, tx, ty, tz, pore, mass, out_ref):
-    step = pl.program_id(0)
-    planes = press.shape[0]
+def pack_columns(step, fields, out_ref):
+    planes = fields[1].shape[0]
     shape = (out_ref.shape[0], LANES)
     lane = lane_of(shape)
 
@@ -136,7 +146,7 @@
         for quarter in range(4):
             index = 4 * tile + quarter
             for z in range(planes if index <= MASS else 0):
-                plane = field_plane(index, z, comp, press, tx, ty, tz, pore, mass)
+                plane = field_plane(index, z, *fields)
                 first, last = plane[:, :LANES], plane[:, -LANES:]
                 at = 32 * quarter + 4 * z
                 both = jnp.where(lane < LANES // 2, first, last)
@@ -146,88 +156,102 @@
         out_ref[:, span] += pltpu.roll(packed, 4 * planes * step, 1)
 
 
-def own_cells(pack, flags, vol, slope, mix, comp, press, pore, mass, *rest):
-    per_tile = 2
-    if pack:
-        tx, ty, tz, mob_ref, acc_ref, mob_sum, acc_sum, low_ref, high_ref, operand = rest
-        tile_row = pl.program_id(0) * (flags.shape[1] // per_tile - 1)
-    else:
-        mob_ref, acc_ref, mob_sum, acc_sum, operand = rest[-5:]
-        tile_row = pl.program_id(0) + 1
+def flash_tiles(tiles, flags, vol, slope, operand, comp, press, pore, mass, mob_ref, acc_ref, mob_sum, acc_sum):
     layer = lax.axis_index("layer")
-    signed, slopes = parameters(vol, slope)
     planes, _, width = press.shape
+    places = [(z, slice(at, at + ROWS), tile) for z in range(planes) for at, tile in tiles]
+
+    def beside(parts):
+        return jnp.concatenate(parts, axis=1)
+
+    def store(ref, value, *lead):
+        for n, (z, at, _) in enumerate(places):
+            ref[(*lead, z, at)] = value[:, n * width : (n + 1) * width]
+
+    def load(ref, *lead):
+        return beside([ref[(*lead, z, at)] for z, at, _ in places])
+
+    raw = [load(comp, i) for i in range(COMPS)]
+    inverse = rcp(total_of(raw))
+    feed = [raw[i] * inverse for i in range(COMPS)]
+    volume = load(pore)
+    acc = [volume * feed[i] - load(mass, i) for i in range(COMPS)]
+    for i in range(COMPS):
+        store(acc_ref, acc[i], i)
+    store(acc_sum, total_of(acc))
+    some = total_of(flags[layer, 2 * tile] + flags[layer, 2 * tile + 1] for _, tile in tiles)
+
+    @pl.when(some > 0)
+    def _():
+        signed, slopes = parameters(vol, slope)
+        two = flash(feed, load(press), signed, slopes, operand[...])
+        row = row_of((ROWS, width))
+        marked = beside(
+            [
+                jnp.where(row < ROWS // 2, flags[layer, 2 * tile], flags[layer, 2 * tile + 1])
+                for _, _, tile in places
+            ]
+        )
+        mobility = [jnp.where(marked > 0, two[i], feed[i]) for i in range(COMPS)]
+        for i in range(COMPS):
+            store(mob_ref, mobility[i], i)
+        store(mob_sum, total_of(mobility))
+
+    @pl.when(some == 0)
+    def _():
+        for i in range(COMPS):
+            store(mob_ref, feed[i], i)
+        store(mob_sum, total_of(feed))
+
+
+def edge_cells(
+    flags, vol, slope, mix, comp, press, tx, ty, tz, pore, mass,
+    mob_ref, acc_ref, mob_sum, acc_sum, packet, low_ref, high_ref, operand,
+):
+    step = pl.program_id(0)
+    planes, rows, width = press.shape
+
+    @pl.when(step == 0)
+    def _():
+        operand[...] = mixing_operand(mix)
+
+    pack_columns(step, (comp, press, tx, ty, tz, pore, mass), packet)
+    ends = ((0, 0), (rows - ROWS, rows // ROWS - 1))
+    flash_tiles(
+        ends, flags, vol, slope, operand, comp, press, pore, mass, mob_ref, acc_ref, mob_sum, acc_sum
+    )
+    rest_fields = {
+        H_MOB: mob_sum, H_PRESS: press, H_TX: tx, H_TY: ty, H_TZ: tz, H_PORE: pore, H_ACC: acc_sum,
+    }
+    half = FIELDS // 2
+    row = row_of((ROWS, width))
+    for k in range(half):
+        for pair in range(planes // 2):
+            near, far = [], []
+            for z in (2 * pair, 2 * pair + 1):
+                here = mob_ref[k, z]
+                beside = rest_fields[k + half][z] if k + half >= COMPS else mob_ref[k + half, z]
+                low, high = here[:ROWS], here[rows - ROWS :]
+                near.append(jnp.where(row % 4 >= 2, pltpu.roll(low, 2, 0), beside[:ROWS]))
+                far.append(
+                    jnp.where(
+                        row % 4 < 2, pltpu.roll(high, 2, 0), pltpu.roll(beside[rows - ROWS :], 4, 0)
+                    )
+                )
+            at = pl.ds(pair * ROWS, ROWS)
+            low_ref[k, at, :] = jnp.where(row < 4, near[0], pltpu.roll(near[1], 4, 0))
+            high_ref[k, at, :] = jnp.where(row < 4, far[0], pltpu.roll(far[1], 4, 0))
+
+
+def inner_cells(start, flags, vol, slope, mix, comp, press, pore, mass, *rest):
+    outs, operand = rest[-5:-1], rest[-1]
 
     @pl.when((pl.program_id(0) == 0) & (pl.program_id(1) == 0))
     def _():
         operand[...] = mixing_operand(mix)
 
-    raw = [comp[i] for i in range(COMPS)]
-    inverse = rcp(total_of(raw))
-    feed = [raw[i] * inverse for i in range(COMPS)]
-    volume = pore[...]
-    acc = [volume * feed[i] - mass[i] for i in range(COMPS)]
-    for i in range(COMPS):
-        acc_ref[i] = acc[i]
-    acc_sum[...] = total_of(acc)
-    tile_flags = [flags[layer, tile_row * per_tile + b] for b in range(per_tile)]
-    some = tile_flags[0] + tile_flags[1]
-
-    @pl.when(some > 0)
-    def _():
-        def beside(x):
-            return jnp.concatenate([x[z] for z in range(planes)], axis=1)
-
-        here = [beside(feed[i]) for i in range(COMPS)]
-        two = flash(here, beside(press), signed, slopes, operand[...])
-        marked = jnp.where(row_of(here[0].shape) < ROWS // per_tile, tile_flags[0], tile_flags[1])
-        mobility = [jnp.where(marked > 0, two[i], here[i]) for i in range(COMPS)]
-        total = total_of(mobility)
-        for z in range(planes):
-            span = slice(z * width, (z + 1) * width)
-            for i in range(COMPS):
-                mob_ref[i, z] = mobility[i][:, span]
-            mob_sum[z] = total[:, span]
-
-    @pl.when(some == 0)
-    def _():
-        for i in range(COMPS):
-            mob_ref[i] = feed[i]
-        mob_sum[...] = total_of(feed)
-
-    if not pack:
-        return
-    rest_fields = {
-        H_MOB: mob_sum, H_PRESS: press, H_TX: tx, H_TY: ty, H_TZ: tz, H_PORE: pore, H_ACC: acc_sum,
-    }
-
-    def field(k, z):
-        return mob_ref[k, z] if k < COMPS else rest_fields[k][z]
-
-    half = FIELDS // 2
-    row = row_of((ROWS, width))
-
-    @pl.when(pl.program_id(0) == 0)
-    def _():
-        for k in range(half):
-            for pair in range(planes // 2):
-                near, far = [
-                    jnp.where(row % 4 >= 2, pltpu.roll(field(k, z), 2, 0), field(k + half, z))
-                    for z in (2 * pair, 2 * pair + 1)
-                ]
-                low_ref[k, pl.ds(pair * ROWS, ROWS), :] = jnp.where(row < 4, near, pltpu.roll(far, 4, 0))
-
-    @pl.when(pl.program_id(0) == 1)
-    def _():
-        for k in range(half):
-            for pair in range(planes // 2):
-                near, far = [
-                    jnp.where(
-                        row % 4 < 2, pltpu.roll(field(k, z), 2, 0), pltpu.roll(field(k + half, z), 4, 0)
-                    )
-                    for z in (2 * pair, 2 * pair + 1)
-                ]
-                high_ref[k, pl.ds(pair * ROWS, ROWS), :] = jnp.where(row < 4, near, pltpu.roll(far, 4, 0))
+    tiles = ((0, pl.program_id(0) + start),)
+    flash_tiles(tiles, flags, vol, slope, operand, comp, press, pore, mass, *outs)
 
 
 def column_cells(flags, vol, slope, mix, left, right, low_in, high_in, out_ref, low_ref, high_ref):
@@ -439,58 +463,53 @@
         pairs = [(i, i + shift) for i in range(count) if 0 <= i + shift < count]
         return lax.ppermute(block, axis, pairs)
 
-    fields = (composition, pressure, trans_x, trans_y, trans_z, pore_volume, mass_old)
-    plane = pl.BlockSpec((PLANES, rows, width), lambda s: (s, 0, 0))
-    planes = pl.BlockSpec((COMPS, PLANES, rows, width), lambda s: (0, s, 0, 0))
-    packet = pl.pallas_call(
-        pack_columns,
-        grid=(depth // PLANES,),
-        in_specs=[planes, plane, plane, plane, plane, plane, planes],
-        out_specs=vmem,
-        out_shape=jax.ShapeDtypeStruct((rows, FIELDS * 32), f32),
-        compiler_params=params(24),
-        name="pack_columns",
-    )(*[pltpu.with_memory_space_constraint(field, pltpu.HBM) for field in fields])
-    left = moved(packet, "layer", 1)
-    right = moved(packet, "layer", -1)
-
     whole = jax.ShapeDtypeStruct((COMPS, depth, rows, width), f32)
     sums = jax.ShapeDtypeStruct((depth, rows, width), f32)
     packed = jax.ShapeDtypeStruct((half + 1, 4 * depth, width), f32)
-    parts = depth // PLANES
     tiles = rows // ROWS
-
-    def own(pack, before):
-        tile_row = (lambda g: g * (tiles - 1)) if pack else (lambda g: g + 1)
-        plane = pl.BlockSpec((PLANES, ROWS, width), lambda g, z: (z, tile_row(g), 0))
-        planes = pl.BlockSpec((COMPS, PLANES, ROWS, width), lambda g, z: (0, z, tile_row(g), 0))
-        block = (half, 4 * PLANES, width)
-        low = pl.BlockSpec(block, lambda g, z: (0, jnp.where(g == 0, z, parts - 1), 0))
-        high = pl.BlockSpec(block, lambda g, z: (0, jnp.where(g == 0, 0, z), 0))
-        count = 2 if pack else tiles - 2
+    operand = pltpu.VMEM((PART, DEEP), jnp.bfloat16)
+    plane = pl.BlockSpec((2, rows, width), lambda s: (s, 0, 0))
+    planes = pl.BlockSpec((COMPS, 2, rows, width), lambda s: (0, s, 0, 0))
+    edge = pl.BlockSpec((half, 2 * 4, width), lambda s: (0, s, 0))
+    fields = (composition, pressure, trans_x, trans_y, trans_z, pore_volume, mass_old)
+    *begun, packet, low, high = pl.pallas_call(
+        edge_cells,
+        grid=(depth // 2,),
+        in_specs=[smem] * 4 + [planes, plane, plane, plane, plane, plane, planes],
+        out_specs=[planes, planes, plane, plane, vmem, edge, edge],
+        out_shape=[
+            whole, whole, sums, sums, jax.ShapeDtypeStruct((rows, FIELDS * 32), f32), packed, packed
+        ],
+        scratch_shapes=[operand],
+        compiler_params=params(24),
+        name="edge_cells",
+    )(*[pltpu.with_memory_space_constraint(x, pltpu.HBM) for x in (*scalars, *fields)])
+    left = moved(packet, "layer", 1)
+    right = moved(packet, "layer", -1)
+
+    def inner(start, count, before):
+        plane = pl.BlockSpec((PLANES, ROWS, width), lambda t, z: (z, start + t, 0))
+        planes = pl.BlockSpec((COMPS, PLANES, ROWS, width), lambda t, z: (0, z, start + t, 0))
         cells = count * ROWS * depth * width
         return pl.pallas_call(
-            functools.partial(own_cells, pack),
-            grid=(count, parts),
+            functools.partial(inner_cells, start),
+            grid=(count, depth // PLANES),
             in_specs=[smem] * 4
             + [planes, plane, plane, planes]
-            + [plane] * (3 if pack else 0)
             + [pl.BlockSpec(memory_space=pl.ANY)] * len(before),
-            out_specs=[planes, planes, plane, plane] + ([low, high] if pack else []),
-            out_shape=[whole, whole, sums, sums] + ([packed, packed] if pack else []),
+            out_specs=[planes, planes, plane, plane],
+            out_shape=[whole, whole, sums, sums],
             input_output_aliases={8 + k: k for k in range(len(before))},
-            scratch_shapes=[pltpu.VMEM((PART, DEEP), jnp.bfloat16)],
+            scratch_shapes=[operand],
             compiler_params=params(24),
             cost_estimate=pl.CostEstimate(
                 flops=900 * cells, transcendentals=190 * cells, bytes_accessed=4 * 39 * cells
             ),
-            name="edge_cells" if pack else "inner_cells",
-        )(
-            *scalars, composition, pressure, pore_volume, mass_old,
-            *((trans_x, trans_y, trans_z) if pack else ()), *before,
-        )
-
-    *begun, low, high = own(True, ())
+            name="inner_cells",
+        )(*scalars, composition, pressure, pore_volume, mass_old, *before)
+
+    early = (tiles - 2) // 2
+    begun = inner(1, early, begun)
 
     left, right, low, high, begun = lax.optimization_barrier((left, right, low, high, begun))
     corner = pl.BlockSpec((1, ROWS, LANES), lambda s: (half, 0, 0))
@@ -507,7 +526,7 @@
     above = moved(high, "areal", 1)
     below = moved(low, "areal", -1)
 
-    mob, acc, mob_sum, acc_sum = own(False, begun)
+    mob, acc, mob_sum, acc_sum = inner(1 + early, tiles - 2 - early, begun)
 
     planes = pl.BlockSpec((COMPS, 2, rows, width), lambda s: (0, s, 0, 0))
     extended = pltpu.VMEM((depth, rows + ROWS, width + LANES), f32)

time: 39.3 us -> 40.6 us (1.033)
  the two profiles are of different devices: /device:TPU:12 before, /device:TPU:11 now
where the time goes in v1:
time: 40.6 us; the launch traced here: 40.4 us
  Pallas kernels  18.1 us (45%)
  starting transfers between devices  16.6 us (41%)
  waiting for transfers between devices  4.76 us (12%)
  between operations  0.87 us (2%)
    ppermute x4, starting transfers between devices, moved(): return lax.ppermute(block, axis, pairs)  16.6 us
    pallas_call x1, Pallas kernels, on_device(): pl.pallas_call(finish, grid=(depth // 2,), in_specs=[vmem] * 12, out_spec...  6.31 us
    pallas_call x2, Pallas kernels, inner(): pl.pallas_call(functools.partial(inner_cells, start), grid=(count, depth...  5.22 us
    pallas_call x1, Pallas kernels, on_device(): pl.pallas_call(edge_cells, grid=(depth // 2,), in_specs=[smem] * 4 + [pla...  4.84 us
    ppermute x4, waiting for transfers between devices, moved(): return lax.ppermute(block, axis, pairs)  4.76 us
    pallas_call x1, Pallas kernels, on_device(): pl.pallas_call(column_cells, grid=(1,), in_specs=[smem] * 4 + [vmem] * 2...  1.73 us
  transfers between devices with their start and end apart: 4, of which 2 were waited for; matrix products, arithmetic and copies ran while one was open for 0% of the time, Pallas kernels for 13%

profile of v1, /device:TPU:11, one launch (start us, length us, event | category | flops | bytes accessed | tf_op | source)
XLA Modules:
  0.0 40.4 jit_solution(17044225071637970176)
XLA Ops:
  0.6 0.0 copy-start.2
  0.6 0.0 copy-start
  0.7 0.0 copy-start.1
  0.7 0.0 copy-start.3
  0.7 0.0 copy-start.9
  0.7 0.0 copy-start.10
  0.7 0.0 copy-start.7
  0.7 0.0 copy-start.8
  0.7 4.8 %edge_cells.1 = (f32[9,8,32,256]{3,2,1,0:T(8,128)S(1)}, f32[9,8,32,256]{3,2,1,0:T(8,128)S(1)}, f32[8,32,256]{2,1,0:T(8,128)S(1)}, f32[8,32,256]{2,1,0:T(8,128)S(...) custom-call(s32[4,8]{1,0:T(4,128)} %flags.7, f32[9]{0:T(128)} %vol.7, f32[9]{0:T(128)} %slope.7, ...), custom_call_target="tpu_custom_call" | custom-call | tf_op jit(solution)/shard_map/edge_cells/pallas_call | solution.py:475
  5.6 7.3 %collective-permute-start = (f32[32,512]{1,0:T(8,128)S(1)}, f32[32,512]{1,0:T(8,128)S(1)}, u32[]{:S(2)}, u32[]{:S(2)}) collective-permute-start(f32[32,512]{1,0:T(8,128)S(1)} %get-tuple-element.28), channel_id=1, source_target_pairs={{0,1},{1,2},{2,3},{4,5},{5,6},{6,7},{8,9},{9,10},{10,11},{12,13},{... | collective-permute-start | bytes 196616 | tf_op jit(solution)/shard_map/ppermute | solution.py:464
  12.9 1.9 %collective-permute-start.1 = (f32[32,512]{1,0:T(8,128)S(1)}, f32[32,512]{1,0:T(8,128)S(1)}, u32[]{:S(2)}, u32[]{:S(2)}) collective-permute-start(f32[32,512]{1,0:T(8,128)S(1)} %get-tuple-element.28), channel_id=1, source_target_pairs={{1,0},{2,1},{3,2},{5,4},{6,5},{7,6},{9,8},{10,9},{11,10},{13,12},{... | collective-permute-start | bytes 196616 | tf_op jit(solution)/shard_map/ppermute | solution.py:464
  14.8 0.0 copy-done.2
  14.8 0.0 copy-done
  14.8 0.0 copy-done.1
  14.8 0.0 copy-done.3
  14.8 0.0 copy-done.9
  14.9 0.0 copy-done.10
  14.9 0.0 copy-done.7
  14.9 1.3 %inner_cells.2 = (f32[9,8,32,256]{3,2,1,0:T(8,128)S(1)}, f32[9,8,32,256]{3,2,1,0:T(8,128)S(1)}, f32[8,32,256]{2,1,0:T(8,128)S(1)}, f32[8,32,256]{2,1,0:T(8,128)S(1)}) custom-call(s32[4,8]{1,0:T(4,128)S(1)} %copy-done.8, f32[9]{0:T(128)S(1)} %copy-done.9, f32[9]{0:T(128)S(1)} %copy-done.10, ...), custom_call_target="tpu_custom_call", output_to_operand_aliasing={{0}: (8, {}), {1}: (9, {}), {2}: (10, {}), {3}: (11, {})} | custom-call | flops 14745600 | bytes 2555904 | tf_op jit(solution)/shard_map/inner_cells/pallas_call | solution.py:494
  16.2 0.0 collective-permute-done.left
  16.2 1.7 %collective-permute-done.1.right = f32[32,512]{1,0:T(8,128)S(1)} collective-permute-done((f32[32,512]{1,0:T(8,128)S(1)}, f32[32,512]{1,0:T(8,128)S(1)}, u32[]{:S(2)}, u32[]{:S(2)}) %collective-permute-start.1) | collective-permute-done | bytes 65568 | tf_op jit(solution)/shard_map/ppermute | solution.py:464
  17.9 1.7 %column_cells.1 = (f32[16,32,128]{2,1,0:T(8,128)S(1)}, f32[9,32,256]{2,1,0:T(8,128)S(1)}, f32[9,32,256]{2,1,0:T(8,128)S(1)}) custom-call(s32[4,8]{1,0:T(4,128)S(1)} %copy-done.8, f32[9]{0:T(128)S(1)} %copy-done.9, f32[9]{0:T(128)S(1)} %copy-done.10, f32[9,9]{1,0:T(8,128)S(1)} %copy-done.7, ...), custom_call_target="tpu_custom_call", output_to_operand_aliasing={{1}: (6, {}), {2}: (7, {})} | custom-call | tf_op jit(solution)/shard_map/column_cells/pallas_call | solution.py:516
  19.6 5.4 %collective-permute-start.2 = (f32[9,32,256]{2,1,0:T(8,128)S(1)}, f32[9,32,256]{2,1,0:T(8,128)S(1)}, u32[]{:S(2)}, u32[]{:S(2)}) collective-permute-start(f32[9,32,256]{2,1,0:T(8,128)S(1)} %get-tuple-element.44), channel_id=1, source_target_pairs={{0,4},{4,8},{8,12},{12,16},{16,20},{20,24},{24,28},{1,5},{5,9},{9,... | collective-permute-start | bytes 884744 | tf_op jit(solution)/shard_map/ppermute | solution.py:464
  25.0 0.0 copy-start.4
  25.0 0.0 copy-start.5
  25.0 0.0 copy-start.6
  25.0 2.1 %collective-permute-start.3 = (f32[9,32,256]{2,1,0:T(8,128)S(1)}, f32[9,32,256]{2,1,0:T(8,128)S(1)}, u32[]{:S(2)}, u32[]{:S(2)}) collective-permute-start(f32[9,32,256]{2,1,0:T(8,128)S(1)} %get-tuple-element.45), channel_id=1, source_target_pairs={{4,0},{8,4},{12,8},{16,12},{20,16},{24,20},{28,24},{5,1},{9,5},{13... | collective-permute-start | bytes 884744 | tf_op jit(solution)/shard_map/ppermute | solution.py:464
  27.1 3.9 %inner_cells.3 = (f32[9,8,32,256]{3,2,1,0:T(8,128)S(1)}, f32[9,8,32,256]{3,2,1,0:T(8,128)S(1)}, f32[8,32,256]{2,1,0:T(8,128)S(1)}, f32[8,32,256]{2,1,0:T(8,128)S(1)}) custom-call(s32[4,8]{1,0:T(4,128)S(1)} %copy-done.8, f32[9]{0:T(128)S(1)} %copy-done.9, f32[9]{0:T(128)S(1)} %copy-done.10, ...), custom_call_target="tpu_custom_call", output_to_operand_aliasing={{0}: (8, {}), {1}: (9, {}), {2}: (10, {}), {3}: (11, {})} | custom-call | flops 14745600 | bytes 2555904 | tf_op jit(solution)/shard_map/inner_cells/pallas_call | solution.py:494
  31.0 0.0 collective-permute-done.2.above
  31.0 3.1 %collective-permute-done.3.below = f32[9,32,256]{2,1,0:T(8,128)S(1)} collective-permute-done((f32[9,32,256]{2,1,0:T(8,128)S(1)}, f32[9,32,256]{2,1,0:T(8,128)S(1)}, u32[]{:S(2)}, u32[]{:S(2)}) %collective-permute-start.3) | collective-permute-done | bytes 294944 | tf_op jit(solution)/shard_map/ppermute | solution.py:464
  34.1 0.0 copy-done.5
  34.1 6.3 %finish.1 = (f32[9,8,32,256]{3,2,1,0:T(8,128)}, f32[8,32,256]{2,1,0:T(8,128)}) custom-call(f32[16,32,128]{2,1,0:T(8,128)S(1)} %get-tuple-element.43.columns, f32[9,32,256]{2,1,0:T(8,128)S(1)} %collective-permute-done.2.above, f32[9,32,256]{2,1,0:T(8,128)S(1)} %collective-permute-done.3.below, f32[8,32,256]{2,1,0:T(8,128)S(1)} %copy-done.2, ...), custom_call_target="tpu_custom_call" | custom-call | tf_op jit(solution)/shard_map/finish/pallas_call | solution.py:534
  (3 shorter events, 0.0 us)
Async XLA Ops:
  0.6 14.2 %copy-start.2 = (f32[8,32,256]{2,1,0:T(8,128)S(1)}, f32[8,32,256]{2,1,0:T(8,128)}, u32[]{:S(2)}) copy-start(f32[8,32,256]{2,1,0:T(8,128)} %press.7) | copy-start | bytes 786436
  0.6 14.2 %copy-start = (f32[9,8,32,256]{3,2,1,0:T(8,128)S(1)}, f32[9,8,32,256]{3,2,1,0:T(8,128)}, u32[]{:S(2)}) copy-start(f32[9,8,32,256]{3,2,1,0:T(8,128)} %comp.5) | copy-start | bytes 7077892
  0.7 14.2 %copy-start.1 = (f32[9,8,32,256]{3,2,1,0:T(8,128)S(1)}, f32[9,8,32,256]{3,2,1,0:T(8,128)}, u32[]{:S(2)}) copy-start(f32[9,8,32,256]{3,2,1,0:T(8,128)} %mass.5) | copy-start | bytes 7077892
  0.7 14.2 %copy-start.3 = (f32[8,32,256]{2,1,0:T(8,128)S(1)}, f32[8,32,256]{2,1,0:T(8,128)}, u32[]{:S(2)}) copy-start(f32[8,32,256]{2,1,0:T(8,128)} %pore.7) | copy-start | bytes 786436
  0.7 14.2 %copy-start.9 = (f32[9]{0:T(128)S(1)}, f32[9]{0:T(128)}, u32[]{:S(2)}) copy-start(f32[9]{0:T(128)} %vol.7) | copy-start | bytes 112
  0.7 14.2 %copy-start.10 = (f32[9]{0:T(128)S(1)}, f32[9]{0:T(128)}, u32[]{:S(2)}) copy-start(f32[9]{0:T(128)} %slope.7) | copy-start | bytes 112
  0.7 14.2 %copy-start.7 = (f32[9,9]{1,0:T(8,128)S(1)}, f32[9,9]{1,0:T(8,128)}, u32[]{:S(2)}) copy-start(f32[9,9]{1,0:T(8,128)} %mix.7) | copy-start | bytes 976
  0.7 14.2 %copy-start.8 = (s32[4,8]{1,0:T(4,128)S(1)}, s32[4,8]{1,0:T(4,128)}, u32[]{:S(2)}) copy-start(s32[4,8]{1,0:T(4,128)} %flags.7) | copy-start | bytes 388
  5.6 10.6 %collective-permute-start = (f32[32,512]{1,0:T(8,128)S(1)}, f32[32,512]{1,0:T(8,128)S(1)}, u32[]{:S(2)}, u32[]{:S(2)}) collective-permute-start(f32[32,512]{1,0:T(8,128)S(1)} %get-tuple-element.28), channel_id=1, source_target_pairs={{0,1},{1,2},{2,3},{4,5},{5,6},{6,7},{8,9},{9,10},{10,11},{12,13},{... | collective-permute-start | bytes 196616 | tf_op jit(solution)/shard_map/ppermute | solution.py:464
  12.9 5.0 %collective-permute-start.1 = (f32[32,512]{1,0:T(8,128)S(1)}, f32[32,512]{1,0:T(8,128)S(1)}, u32[]{:S(2)}, u32[]{:S(2)}) collective-permute-start(f32[32,512]{1,0:T(8,128)S(1)} %get-tuple-element.28), channel_id=1, source_target_pairs={{1,0},{2,1},{3,2},{5,4},{6,5},{7,6},{9,8},{10,9},{11,10},{13,12},{... | collective-permute-start | bytes 196616 | tf_op jit(solution)/shard_map/ppermute | solution.py:464
  19.6 11.4 %collective-permute-start.2 = (f32[9,32,256]{2,1,0:T(8,128)S(1)}, f32[9,32,256]{2,1,0:T(8,128)S(1)}, u32[]{:S(2)}, u32[]{:S(2)}) collective-permute-start(f32[9,32,256]{2,1,0:T(8,128)S(1)} %get-tuple-element.44), channel_id=1, source_target_pairs={{0,4},{4,8},{8,12},{12,16},{16,20},{20,24},{24,28},{1,5},{5,9},{9,... | collective-permute-start | bytes 884744 | tf_op jit(solution)/shard_map/ppermute | solution.py:464
  25.0 9.1 %copy-start.4 = (f32[8,32,256]{2,1,0:T(8,128)S(1)}, f32[8,32,256]{2,1,0:T(8,128)}, u32[]{:S(2)}) copy-start(f32[8,32,256]{2,1,0:T(8,128)} %tx.3) | copy-start | bytes 786436
  25.0 9.1 %copy-start.5 = (f32[8,32,256]{2,1,0:T(8,128)S(1)}, f32[8,32,256]{2,1,0:T(8,128)}, u32[]{:S(2)}) copy-start(f32[8,32,256]{2,1,0:T(8,128)} %ty.3) | copy-start | bytes 786436
  25.0 9.1 %copy-start.6 = (f32[8,32,256]{2,1,0:T(8,128)S(1)}, f32[8,32,256]{2,1,0:T(8,128)}, u32[]{:S(2)}) copy-start(f32[8,32,256]{2,1,0:T(8,128)} %tz.3) | copy-start | bytes 786436
  25.0 9.1 %collective-permute-start.3 = (f32[9,32,256]{2,1,0:T(8,128)S(1)}, f32[9,32,256]{2,1,0:T(8,128)S(1)}, u32[]{:S(2)}, u32[]{:S(2)}) collective-permute-start(f32[9,32,256]{2,1,0:T(8,128)S(1)} %get-tuple-element.45), channel_id=1, source_target_pairs={{4,0},{8,4},{12,8},{16,12},{20,16},{24,20},{28,24},{5,1},{9,5},{13... | collective-permute-start | bytes 884744 | tf_op jit(solution)/shard_map/ppermute | solution.py:464

commit v2 on v0

v2 whole, which is shorter than its diff:
```python
import functools

import jax
import jax.numpy as jnp
from jax import lax
from jax.experimental import pallas as pl
from jax.experimental.pallas import tpu as pltpu
from jax.sharding import PartitionSpec as P

SS_ITERS = 3
RR_ITERS = 3
LIGHT = 4
COMPS = 9
FIELDS = 16
MOB, PRESS, TX, TY, TZ, PORE, ACC = range(COMPS, FIELDS)
UNITS = (MOB, PRESS, TX, (0, 1), (2, 3), (4, 5), (6, 7), (8, TY), (TZ, PORE), (ACC, ACC))
DEPTH_SLOTS = 4
TIME_STEP = 4.0
COMPRESS = 0.2
VAPOUR_WEIGHT = 1.0 / 0.25
LANES = 128
ROWS = 8
MIB = 1024 * 1024
PART = (COMPS + 1) * ROWS
DEEP = 256
PLANES = 4


def rcp(x):
    return pltpu.reciprocal(x, approx=True)


def total_of(terms):
    terms = list(terms)
    while len(terms) > 1:
        terms = [a + b for a, b in zip(terms[::2], terms[1::2])] + (
            [terms[-1]] if len(terms) % 2 else []
        )
    return terms[0]


def split(x):
    high = x.astype(jnp.bfloat16)
    return high, (x - high.astype(jnp.float32)).astype(jnp.bfloat16)


def mixing_operand(mix_ref):
    shape = (ROWS, DEEP)
    lane, row = lane_of(shape), row_of(shape)
    part = lax.div(lane, PART)
    within = lane - PART * part
    column = lax.div(within, ROWS)
    on = (within - ROWS * column == row) & (part < 3)
    blocks = []
    for i in range(COMPS):
        value = jnp.zeros(shape, jnp.float32)
        for j in range(COMPS):
            value = jnp.where(column == j, 2.0 * mix_ref[i, j], value)
        high, low = split(value)
        value = jnp.where(part == 2, low.astype(jnp.float32), high.astype(jnp.float32))
        blocks.append(jnp.where(on, value, 0.0))
    blocks.append(jnp.zeros(shape, jnp.float32))
    return jnp.concatenate(blocks, axis=0).astype(jnp.bfloat16)


def mixed(operand, spread):
    shape = spread[0].shape
    high, low = split(jnp.concatenate(spread + [jnp.zeros(shape, jnp.float32)], axis=0))
    tail = jnp.zeros((DEEP - 3 * PART, shape[1]), jnp.bfloat16)
    out = jnp.dot(
        operand,
        jnp.concatenate([high, low, high, tail], axis=0),
        preferred_element_type=jnp.float32,
    )
    return [out[ROWS * i : ROWS * (i + 1)] for i in range(COMPS)]


def flash(feed, pressure, signed, slope, operand):
    log_press = jnp.log(pressure)
    half_base = [0.5 * signed[i] - (0.5 * slope[i]) * log_press for i in range(COMPS)]
    spread = None
    for outer in range(SS_ITERS):
        if outer == 0:
            half_log = half_base
        else:
            mix = mixed(operand, spread)
            half_log = [half_base[i] - 0.5 * jnp.tanh(mix[i]) for i in range(COMPS)]
        t = [jnp.tanh(half_log[i]) for i in range(COMPS)]
        u = [rcp(t[i]) for i in range(COMPS)]
        psi = None
        for inner in range(RR_ITERS):
            q = t if inner == 0 else [rcp(u[i] + psi) for i in range(COMPS)]
            part = [feed[i] * q[i] for i in range(COMPS)]
            step = total_of(part) * rcp(total_of(part[i] * q[i] for i in range(COMPS)))
            psi = jnp.clip(step if inner == 0 else psi + step, -1.0, 1.0)
        spread = [feed[i] * rcp(u[i] + psi) for i in range(COMPS)]
    liquid_part = (0.25 * (1.0 - psi)) * (1.0 - psi)
    vapour_part = (0.25 * VAPOUR_WEIGHT * (1.0 + psi)) * (1.0 + psi)
    both, apart = vapour_part + liquid_part, vapour_part - liquid_part
    return [spread[i] * (both * u[i] + apart) for i in range(COMPS)]


def parameters(vol_ref, slope_ref):
    signed = [vol_ref[i] if i < LIGHT else -vol_ref[i] for i in range(COMPS)]
    return signed, [slope_ref[i] for i in range(COMPS)]


def lane_of(shape):
    return lax.broadcasted_iota(jnp.int32, shape, len(shape) - 1)


def row_of(shape):
    return lax.broadcasted_iota(jnp.int32, shape, len(shape) - 2)


def pack_rows(field, low_ref, high_ref, planes):
    row = None
    for n in range(0, len(UNITS), 2):
        lows, highs = [], []
        for z in range(planes):
            for unit in UNITS[n : n + 2]:
                if isinstance(unit, tuple):
                    (first_a, last_a), (first_b, last_b) = (field(k, z) for k in unit)
                    if row is None:
                        row = row_of(first_a.shape)
                    low = jnp.where(row == 2, pltpu.roll(first_a, 2, 0), pltpu.roll(first_b, 3, 0))
                    high = jnp.where(row == 0, pltpu.roll(last_b, 1, 0), pltpu.roll(last_a, 2, 0))
                else:
                    first, last = field(unit, z)
                    if row is None:
                        row = row_of(first.shape)
                    low, high = pltpu.roll(first, 2, 0), pltpu.roll(last, 2, 0)
                lows.append(low)
                highs.append(high)
        for pair in range(planes // 2):
            at = pl.ds(pair * ROWS, ROWS)
            l, h = lows[4 * pair : 4 * pair + 4], highs[4 * pair : 4 * pair + 4]
            if low_ref is not None:
                low_ref[n // 2, at, :] = jnp.where(
                    row < 4,
                    jnp.where(row >= 2, l[0], pltpu.roll(l[1], 6, 0)),
                    jnp.where(row >= 6, pltpu.roll(l[2], 4, 0), pltpu.roll(l[3], 2, 0)),
                )
            if high_ref is not None:
                high_ref[n // 2, at, :] = jnp.where(
                    row < 4,
                    jnp.where(row < 2, h[0], pltpu.roll(h[1], 2, 0)),
                    jnp.where(row < 6, pltpu.roll(h[2], 4, 0), pltpu.roll(h[3], 6, 0)),
                )


def row_tiles(above, below, wanted):
    shape = above.shape[1:]
    upper = row_of(shape) % DEPTH_SLOTS < 2
    tile_row = row_of((ROWS, shape[1]))
    depth = shape[0] // DEPTH_SLOTS
    tiles = {}
    for n, unit in enumerate(UNITS):
        fields = unit if isinstance(unit, tuple) else (unit,)
        if not any(k in wanted for k in fields):
            continue
        up, down = above[n // 2], below[n // 2]
        if n % 2:
            up, down = pltpu.roll(up, shape[0] - 2, 0), pltpu.roll(down, 2, 0)
        both = jnp.where(upper, up, down)
        for z in range(depth):
            at = (z // 2) * ROWS
            tile = pltpu.roll(both[at : at + ROWS], 6 - 4 * (z % 2), 0)
            if fields[0] in wanted:
                tiles.setdefault(fields[0], []).append(tile)
            if fields[-1] in wanted and fields[-1] != fields[0]:
                other = jnp.where(tile_row < 4, pltpu.roll(tile, ROWS - 1, 0), pltpu.roll(tile, 1, 0))
                tiles.setdefault(fields[-1], []).append(other)
    return tiles


def pack_columns(above, below, mob, mob_sum, press, tx, ty, tz, pore, acc_sum, out_ref):
    depth, rows, width = press.shape
    shape = (rows + ROWS, LANES)
    lane = lane_of(shape)
    corner_fields = {MOB: mob_sum, PRESS: press, TX: tx, TY: ty}
    others = {TZ: tz, PORE: pore, ACC: acc_sum, **corner_fields}
    corners = row_tiles(above, below, corner_fields)
    nothing = jnp.zeros((ROWS, LANES), jnp.float32)
    for tile in range(FIELDS // 4):
        packed = jnp.zeros(shape, jnp.float32)
        for quarter in range(4):
            k = 4 * tile + quarter
            for z in range(depth):
                plane = mob[k, z] if k < COMPS else others[k][z]
                first, last = plane[:, :LANES], plane[:, -LANES:]
                at = 32 * quarter + 4 * z
                if k < COMPS:
                    one = pltpu.roll(jnp.concatenate([first, nothing], axis=0), at + 1, 1)
                    two = pltpu.roll(jnp.concatenate([last, nothing], axis=0), (at + 3) % LANES, 1)
                    packed = jnp.where(lane == at + 1, one, jnp.where(lane == at + 2, two, packed))
                    continue
                both = jnp.where(lane_of(first.shape) < LANES // 2, first, last)
                end = nothing
                if k in corner_fields:
                    end = corners[k][z]
                    end = jnp.where(lane_of(end[:, :LANES].shape) < LANES // 2, end[:, :LANES], end[:, -LANES:])
                both = pltpu.roll(jnp.concatenate([both, end], axis=0), (at + 2) % LANES, 1)
                packed = jnp.where((lane >= at) & (lane < at + 4), both, packed)
        out_ref[:, tile * LANES : (tile + 1) * LANES] = packed


def side_fields(left, right):
    fields = []
    lane = lane_of((left.shape[0], LANES))
    for tile in range(FIELDS // 4):
        span = slice(tile * LANES, (tile + 1) * LANES)
        l, r = left[:, span], right[:, span]
        one = jnp.where(lane % 4 < 2, r, l)
        other = jnp.where(lane % 4 < 2, l, r)
        for quarter in range(4):
            turn = (LANES - 32 * quarter) % LANES
            both = one if 4 * tile + quarter < COMPS else other
            fields.append(pltpu.roll(both, turn, 1) if turn else both)
    return fields


def own_cells(pack, flags, vol, slope, mix, comp, press, pore, mass, *rest):
    per_tile = 2
    if pack:
        tx, ty, tz, mob_ref, acc_ref, mob_sum, acc_sum, low_ref, high_ref, operand = rest
        tile_row = pl.program_id(0) * (flags.shape[1] // per_tile - 1)
    else:
        mob_ref, acc_ref, mob_sum, acc_sum, operand = rest[-5:]
        tile_row = pl.program_id(0) + 1
    layer = lax.axis_index("layer")
    signed, slopes = parameters(vol, slope)
    planes, _, width = press.shape

    @pl.when((pl.program_id(0) == 0) & (pl.program_id(1) == 0))
    def _():
        operand[...] = mixing_operand(mix)

    raw = [comp[i] for i in range(COMPS)]
    inverse = rcp(total_of(raw))
    feed = [raw[i] * inverse for i in range(COMPS)]
    volume = pore[...]
    acc = [volume * feed[i] - mass[i] for i in range(COMPS)]
    for i in range(COMPS):
        acc_ref[i] = acc[i]
    acc_sum[...] = total_of(acc)
    tile_flags = [flags[layer, tile_row * per_tile + b] for b in range(per_tile)]
    some = tile_flags[0] + tile_flags[1]

    @pl.when(some > 0)
    def _():
        def beside(x):
            return jnp.concatenate([x[z] for z in range(planes)], axis=1)

        here = [beside(feed[i]) for i in range(COMPS)]
        two = flash(here, beside(press), signed, slopes, operand[...])
        marked = jnp.where(row_of(here[0].shape) < ROWS // per_tile, tile_flags[0], tile_flags[1])
        mobility = [jnp.where(marked > 0, two[i], here[i]) for i in range(COMPS)]
        total = total_of(mobility)
        for z in range(planes):
            span = slice(z * width, (z + 1) * width)
            for i in range(COMPS):
                mob_ref[i, z] = mobility[i][:, span]
            mob_sum[z] = total[:, span]

    @pl.when(some == 0)
    def _():
        for i in range(COMPS):
            mob_ref[i] = feed[i]
        mob_sum[...] = total_of(feed)

    if not pack:
        return
    rest_fields = {
        MOB: mob_sum, PRESS: press, TX: tx, TY: ty, TZ: tz, PORE: pore, ACC: acc_sum,
    }

    def field(k, z):
        here = mob_ref[k, z] if k < COMPS else rest_fields[k][z]
        return here, here

    @pl.when(pl.program_id(0) == 0)
    def _():
        pack_rows(field, low_ref, None, planes)

    @pl.when(pl.program_id(0) == 1)
    def _():
        pack_rows(field, None, high_ref, planes)


def near_residual(above, below, press, tx, ty, tz, mob, acc, out_ref, rows_h, press_h, tx_h):
    step = pl.program_id(0)
    planes = out_ref.shape[1]
    depth, rows, width = press.shape
    areal, areals = lax.axis_index("areal"), lax.axis_size("areal")
    tall = rows + ROWS

    @pl.when(step == 0)
    def _():
        tiles = row_tiles(above, below, (PRESS, TX, *range(COMPS)))
        for z in range(depth):
            press_h[z] = tiles[PRESS][z]
            tx_h[z] = tiles[TX][z]
            for i in range(COMPS):
                rows_h[i, z] = tiles[i][z]

    own = slice(0, rows)
    scale = 0.5 * TIME_STEP
    end_x = (row_of((tall, width)) == rows - 1) & (areal == areals - 1)
    end_y = lane_of((rows, width)) == width - 1
    for plane in range(planes):
        z = step * planes + plane
        down, up = jnp.maximum(z - 1, 0), jnp.minimum(z + 1, depth - 1)
        p = press[z]
        p_tall = jnp.concatenate([p, press_h[z]], axis=0)
        t_tall = jnp.where(end_x, 0.0, scale * jnp.concatenate([tx[z], tx_h[z]], axis=0))
        gx = t_tall * (p_tall - pltpu.roll(p_tall, tall - 1, 0))
        gx_low = -pltpu.roll(gx, 1, 0)[own]
        gx = gx[own]
        gy = jnp.where(end_y, 0.0, scale * ty[z]) * (p - pltpu.roll(p, width - 1, 1))
        gy_low = -pltpu.roll(gy, 1, 1)
        gz = jnp.where(z < depth - 1, scale, 0.0) * tz[z] * (p - press[up])
        gz_low = jnp.where(z > 0, scale, 0.0) * tz[down] * (p - press[down])
        middle = (gx + gx_low) + (gy + gy_low) + (gz + gz_low)
        for i in range(COMPS):
            here = mob[i, z]
            tall_here = jnp.concatenate([here, rows_h[i, z]], axis=0)
            out_ref[i, plane] = (
                acc[i, z]
                + middle * here
                + gx * pltpu.roll(tall_here, tall - 1, 0)[own]
                + gx_low * pltpu.roll(tall_here, 1, 0)[own]
                + gy * pltpu.roll(here, width - 1, 1)
                + gy_low * pltpu.roll(here, 1, 1)
                + gz * mob[i, up]
                + gz_low * mob[i, down]
            )


def finish(
    left, right, above, below,
    press, tx, ty, tz, pore, mob_sum, acc_sum, mob, near,
    res_ref, new_ref,
    side_h, e_press, e_tx, e_ty, e_tz, e_pore, e_mob, e_acc,
    c_x, c_y, c_z, first, g_first, g_last,
):
    step = pl.program_id(0)
    planes = res_ref.shape[1]
    depth, rows, width = press.shape
    layer, layers = lax.axis_index("layer"), lax.axis_size("layer")
    areal, areals = lax.axis_index("areal"), lax.axis_size("areal")
    tall, wide = rows + ROWS, width + LANES
    full = (tall, wide)
    own = (slice(0, rows), slice(0, width))

    @pl.when(step == 0)
    def _():
        extended = {
            MOB: (e_mob, mob_sum), PRESS: (e_press, press), TX: (e_tx, tx), TY: (e_ty, ty),
            TZ: (e_tz, tz), PORE: (e_pore, pore), ACC: (e_acc, acc_sum),
        }
        tiles = row_tiles(above, below, extended)
        columns = side_fields(left, right)
        for i in range(COMPS):
            side_h[i] = columns[i][:rows]
        for k, (e_ref, own_ref) in extended.items():
            for z in range(depth):
                e_ref[z, pl.ds(0, rows), pl.ds(0, width)] = own_ref[z]
                e_ref[z, pl.ds(rows, ROWS), pl.ds(0, width)] = tiles[k][z]
                e_ref[z, :, pl.ds(width, LANES)] = pltpu.roll(columns[k], LANES - 2 - 4 * z, 1)

        end_x = (row_of(full) == rows - 1) & (areal == areals - 1)
        end_y = (lane_of(full) == width - 1) & (layer == layers - 1)
        scale = 0.5 * TIME_STEP
        lane = lane_of((rows, LANES))
        c_z[0] = jnp.zeros(full, jnp.float32)

        def update(z):
            p, m = e_press[z], e_mob[z]
            up, down = jnp.minimum(z + 1, depth - 1), jnp.maximum(z - 1, 0)
            strength_x = jnp.where(end_x, 0.0, scale * e_tx[z])
            strength_y = jnp.where(end_y, 0.0, scale * e_ty[z])
            strength_z = jnp.where(z < depth - 1, scale, 0.0) * e_tz[z]
            dx = p - pltpu.roll(p, tall - 1, 0)
            dy = p - pltpu.roll(p, wide - 1, 1)
            dz = p - e_press[up]
            cx = strength_x * (m + pltpu.roll(m, tall - 1, 0))
            cy = strength_y * (m + pltpu.roll(m, wide - 1, 1))
            cz = strength_z * (m + e_mob[up])
            cz_low = c_z[z]
            gy = (strength_y * dy)[:rows]
            g_first[z] = jnp.where(lane == 0, -pltpu.roll(gy[:, width:], 1, 1), 0.0)
            g_last[z] = jnp.where(lane == LANES - 1, gy[:, width - LANES : width], 0.0)
            c_x[z], c_y[z], c_z[z + 1] = cx, cy, cz
            fx, fy = cx * dx, cy * dy
            total = (
                e_acc[z]
                + (fx - pltpu.roll(fx, 1, 0))
                + (fy - pltpu.roll(fy, 1, 1))
                + (cz * dz + cz_low * (p - e_press[down]))
            )
            diagonal = (
                COMPRESS * e_pore[z]
                + (cx + pltpu.roll(cx, 1, 0))
                + (cy + pltpu.roll(cy, 1, 1))
                + (cz + cz_low)
            )
            inverse = rcp(jnp.where(diagonal > 0.0, diagonal, 1.0))
            first[z] = jnp.where(diagonal > 0.0, -total * inverse, 0.0)
            e_acc[z] = total
            e_pore[z] = inverse

        def second(z):
            here = first[z]
            up, down = jnp.minimum(z + 1, depth - 1), jnp.maximum(z - 1, 0)
            cx, cy = c_x[z], c_y[z]
            gathered = (
                (cx * pltpu.roll(here, tall - 1, 0))[own]
                + pltpu.roll(cx * here, 1, 0)[own]
                + (cy * pltpu.roll(here, wide - 1, 1))[own]
                + pltpu.roll(cy * here, 1, 1)[own]
                + (c_z[z + 1] * first[up] + c_z[z] * first[down])[own]
                - e_acc[z][own]
            )
            new_ref[z] = e_press[z][own] + gathered * e_pore[z][own]

        for body in (update, second):
            def pair(t, carry):
                body(2 * t)
                body(2 * t + 1)
                return carry

            lax.fori_loop(0, depth // 2, pair, 0)

    low, high = slice(0, LANES), slice(width - LANES, width)
    for plane in range(planes):
        z = step * planes + plane
        for i in range(COMPS):
            side = pltpu.roll(side_h[i], LANES - 2 - 4 * z, 1)
            here = mob[i, z]
            for span, face in ((low, g_first[z]), (high, g_last[z])):
                res_ref[i, plane, :, span] = near[i, plane, :, span] + face * (here[:, span] + side)


def on_device(
    pressure, composition, mass_old, pore_volume, trans_x, trans_y, trans_z,
    volatility, pressure_slope, mixing, two_phase,
):
    depth, rows, width = pressure.shape
    f32 = jnp.float32
    smem = pl.BlockSpec(memory_space=pltpu.SMEM)
    vmem = pl.BlockSpec(memory_space=pltpu.VMEM)
    def params(mib):
        return pltpu.CompilerParams(vmem_limit_bytes=mib * MIB)

    scalars = (two_phase, volatility, pressure_slope, mixing)

    def moved(block, axis, shift):
        count = lax.axis_size(axis)
        pairs = [(i, i + shift) for i in range(count) if 0 <= i + shift < count]
        return lax.ppermute(block, axis, pairs)

    whole = jax.ShapeDtypeStruct((COMPS, depth, rows, width), f32)
    sums = jax.ShapeDtypeStruct((depth, rows, width), f32)
    packed = jax.ShapeDtypeStruct((len(UNITS) // 2, DEPTH_SLOTS * depth, width), f32)
    parts = depth // PLANES
    tiles = rows // ROWS

    fields = (composition, pressure, pore_volume, mass_old, trans_x, trans_y, trans_z)

    def pinned(x):
        return pltpu.with_memory_space_constraint(x, pltpu.HBM)

    def own(pack, before):
        tile_row = (lambda g: g * (tiles - 1)) if pack else (lambda g: g + 1)
        plane = pl.BlockSpec((PLANES, ROWS, width), lambda g, z: (z, tile_row(g), 0))
        planes = pl.BlockSpec((COMPS, PLANES, ROWS, width), lambda g, z: (0, z, tile_row(g), 0))
        block = (len(UNITS) // 2, DEPTH_SLOTS * PLANES, width)
        low = pl.BlockSpec(block, lambda g, z: (0, jnp.where(g == 0, z, parts - 1), 0))
        high = pl.BlockSpec(block, lambda g, z: (0, jnp.where(g == 0, 0, z), 0))
        count = 2 if pack else tiles - 2
        cells = count * ROWS * depth * width
        return pl.pallas_call(
            functools.partial(own_cells, pack),
            grid=(count, parts),
            in_specs=[smem] * 4
            + [planes, plane, plane, planes]
            + [plane] * (3 if pack else 0)
            + [pl.BlockSpec(memory_space=pl.ANY)] * len(before),
            out_specs=[planes, planes, plane, plane] + ([low, high] if pack else []),
            out_shape=[whole, whole, sums, sums] + ([packed, packed] if pack else []),
            input_output_aliases={8 + k: k for k in range(len(before))},
            scratch_shapes=[pltpu.VMEM((PART, DEEP), jnp.bfloat16)],
            compiler_params=params(24),
            cost_estimate=pl.CostEstimate(
                flops=900 * cells, transcendentals=190 * cells, bytes_accessed=4 * 39 * cells
            ),
            name="edge_cells" if pack else "inner_cells",
        )(*(pinned(x) if pack else x for x in (*scalars, *fields[: None if pack else 4])), *before)

    *begun, low, high = own(True, ())

    above = moved(high, "areal", 1)
    below = moved(low, "areal", -1)
    mob, acc, mob_sum, acc_sum = own(False, begun)

    packet = pl.pallas_call(
        pack_columns,
        in_specs=[vmem] * 10,
        out_specs=vmem,
        out_shape=jax.ShapeDtypeStruct((rows + ROWS, FIELDS * 32), f32),
        compiler_params=params(24),
        name="pack_columns",
    )(above, below, mob, mob_sum, pressure, trans_x, trans_y, trans_z, pore_volume, acc_sum)
    left = moved(packet, "layer", 1)
    right = moved(packet, "layer", -1)
    planes = pl.BlockSpec((COMPS, 2, rows, width), lambda s: (0, s, 0, 0))
    row_tile = pltpu.VMEM((depth, ROWS, width), f32)
    cells = rows * depth * width
    near = pl.pallas_call(
        near_residual,
        grid=(depth // 2,),
        in_specs=[vmem] * 8,
        out_specs=planes,
        out_shape=whole,
        scratch_shapes=[pltpu.VMEM((COMPS, depth, ROWS, width), f32), row_tile, row_tile],
        compiler_params=params(24),
        cost_estimate=pl.CostEstimate(flops=150 * cells, transcendentals=0, bytes_accessed=4 * 31 * cells),
        name="near_residual",
    )(above, below, pressure, trans_x, trans_y, trans_z, mob, acc)

    extended = pltpu.VMEM((depth, rows + ROWS, width + LANES), f32)
    side = pltpu.VMEM((depth, rows, LANES), f32)
    return pl.pallas_call(
        finish,
        grid=(depth // 2,),
        in_specs=[vmem] * 12 + [planes],
        out_specs=[planes, vmem],
        out_shape=[whole, sums],
        scratch_shapes=[
            pltpu.VMEM((COMPS, rows, LANES), f32),
            *[extended] * 9,
            pltpu.VMEM((depth + 1, rows + ROWS, width + LANES), f32),
            extended,
            side,
            side,
        ],
        compiler_params=params(28),
        name="finish",
    )(
        left, right, above, below,
        pressure, trans_x, trans_y, trans_z, pore_volume, mob_sum, acc_sum, mob, near,
    )


def solution(mesh):
    placed = (
        P(None, "areal", "layer"),
        P(None, None, "areal", "layer"),
        P(None, None, "areal", "layer"),
        P(None, "areal", "layer"),
        P(None, "areal", "layer"),
        P(None, "areal", "layer"),
        P(None, "areal", "layer"),
        P(),
        P(),
        P(),
        P(None, "areal"),
    )
    return jax.shard_map(
        on_device,
        mesh=mesh,
        in_specs=placed,
        out_specs=(P(None, None, "areal", "layer"), P(None, "areal", "layer")),
        check_vma=False,
    )
```

time: 39.3 us -> 35.4 us (0.901)
  Pallas kernels: 25.7 us -> 18.2 us
  starting transfers between devices: 12.4 us -> 14.4 us
  waiting for transfers between devices: 0.01 us -> 1.61 us
    pallas_call x2, Pallas kernels: 14.2 us -> 9.75 us  [own(): pl.pallas_call(functools.partial(own_cells, pack), grid=(count, parts), i...]
    pallas_call x3, Pallas kernels: 11.5 us -> 8.49 us  [the longest x1 4.64 us: on_device(): pl.pallas_call(finish, grid=(depth // 2,), in_specs=[vmem] * 12 + [planes...]
    ppermute x4, starting transfers between devices: 12.4 us -> 14.4 us  [moved(): return lax.ppermute(block, axis, pairs)]
    ppermute x4, waiting for transfers between devices: 0.01 us -> 1.61 us  [moved(): return lax.ppermute(block, axis, pairs)]
  transfers between devices with their start and end apart: 4 -> 4, of which waited for: 0 -> 1; matrix products, arithmetic and copies ran while one was open for 0% -> 0% of each run, Pallas kernels for 36% -> 20%
where the time goes in v2:
time: 35.4 us; the launch traced here: 35.2 us
  Pallas kernels  18.2 us (51%)
  starting transfers between devices  14.4 us (41%)
  waiting for transfers between devices  1.61 us (5%)
  between operations  0.89 us (3%)
    ppermute x4, starting transfers between devices, moved(): return lax.ppermute(block, axis, pairs)  14.4 us
    pallas_call x2, Pallas kernels, own(): pl.pallas_call(functools.partial(own_cells, pack), grid=(count, parts), i...  9.75 us
    pallas_call x1, Pallas kernels, on_device(): pl.pallas_call(finish, grid=(depth // 2,), in_specs=[vmem] * 12 + [planes...  4.64 us
    pallas_call x1, Pallas kernels, on_device(): pl.pallas_call(near_residual, grid=(depth // 2,), in_specs=[vmem] * 8, ou...  2.79 us
    ppermute x4, waiting for transfers between devices, moved(): return lax.ppermute(block, axis, pairs)  1.61 us
    pallas_call x1, Pallas kernels, on_device(): pl.pallas_call(pack_columns, in_specs=[vmem] * 10, out_specs=vmem, out_sh...  1.06 us
  transfers between devices with their start and end apart: 4, of which 1 were waited for; matrix products, arithmetic and copies ran while one was open for 0% of the time, Pallas kernels for 20%

profile of v2, /device:TPU:12, one launch (start us, length us, event | category | flops | bytes accessed | tf_op | source)
XLA Modules:
  0.0 35.2 jit_solution(13719719351066075193)
XLA Ops:
  0.6 0.0 copy-start
  0.6 0.0 copy-start.4
  0.7 0.0 copy-start.8
  0.7 0.0 copy-start.7
  0.7 0.0 copy-start.10
  0.7 0.0 copy-start.9
  0.7 0.0 copy-start.6
  0.7 0.0 copy-start.5
  0.7 5.6 %edge_cells.1 = (f32[9,8,32,256]{3,2,1,0:T(8,128)S(1)}, f32[9,8,32,256]{3,2,1,0:T(8,128)S(1)}, f32[8,32,256]{2,1,0:T(8,128)S(1)}, f32[8,32,256]{2,1,0:T(8,128)S(...) custom-call(s32[4,8]{1,0:T(4,128)} %flags.3, f32[9]{0:T(128)} %vol.3, f32[9]{0:T(128)} %slope.3, f32[9,9]{1,0:T(8,128)} %mix.3, ...), custom_call_target="tpu_custom_call" | custom-call | flops 29491200 | bytes 5111808 | tf_op jit(solution)/shard_map/edge_cells/pallas_call | solution.py:483
  6.4 1.9 %collective-permute-start = (f32[5,32,256]{2,1,0:T(8,128)S(1)}, f32[5,32,256]{2,1,0:T(8,128)S(1)}, u32[]{:S(2)}, u32[]{:S(2)}) collective-permute-start(f32[5,32,256]{2,1,0:T(8,128)S(1)} %get-tuple-element.12), channel_id=1, source_target_pairs={{0,4},{4,8},{8,12},{12,16},{16,20},{20,24},{24,28},{1,5},{5,9},{9,... | collective-permute-start | bytes 491528 | tf_op jit(solution)/shard_map/ppermute | solution.py:461
  8.3 4.5 %collective-permute-start.1 = (f32[5,32,256]{2,1,0:T(8,128)S(1)}, f32[5,32,256]{2,1,0:T(8,128)S(1)}, u32[]{:S(2)}, u32[]{:S(2)}) collective-permute-start(f32[5,32,256]{2,1,0:T(8,128)S(1)} %get-tuple-element.13), channel_id=1, source_target_pairs={{4,0},{8,4},{12,8},{16,12},{20,16},{24,20},{28,24},{5,1},{9,5},{13... | collective-permute-start | bytes 491528 | tf_op jit(solution)/shard_map/ppermute | solution.py:461
  12.8 0.0 copy-done
  12.8 0.0 copy-done.4
  12.9 0.0 copy-done.8
  12.9 0.0 copy-done.7
  12.9 0.0 copy-done.10
  12.9 0.0 copy-done.9
  12.9 0.0 copy-done.6
  12.9 0.0 copy-done.5
  12.9 0.0 copy-start.1
  12.9 0.0 copy-start.2
  12.9 0.0 copy-start.3
  12.9 4.1 %inner_cells.1 = (f32[9,8,32,256]{3,2,1,0:T(8,128)S(1)}, f32[9,8,32,256]{3,2,1,0:T(8,128)S(1)}, f32[8,32,256]{2,1,0:T(8,128)S(1)}, f32[8,32,256]{2,1,0:T(8,128)S(1)}) custom-call(s32[4,8]{1,0:T(4,128)S(1)} %copy-done.8, f32[9]{0:T(128)S(1)} %copy-done.9, f32[9]{0:T(128)S(1)} %copy-done.10, ...), custom_call_target="tpu_custom_call", output_to_operand_aliasing={{0}: (8, {}), {1}: (9, {}), {2}: (10, {}), {3}: (11, {})} | custom-call | flops 29491200 | bytes 5111808 | tf_op jit(solution)/shard_map/inner_cells/pallas_call | solution.py:483
  17.1 0.0 collective-permute-done.above
  17.1 0.0 collective-permute-done.1.below
  17.1 1.1 %pack_columns.1 = f32[40,512]{1,0:T(8,128)S(1)} custom-call(f32[5,32,256]{2,1,0:T(8,128)S(1)} %collective-permute-done.above, f32[5,32,256]{2,1,0:T(8,128)S(1)} %collective-permute-done.1.below, f32[9,8,32,256]{3,2,1,0:T(8,128)S(1)} %get-tuple-element.18.mob, f32[8,32,256]{2,1,0:T(8,128)S(1)} %get-tuple-element.19.mob_sum, f32[8,32,256]{2,1,0:T(8,128)S(1)} %copy-done, ...), custom_call_target="tpu_custom_call" | custom-call | tf_op jit(solution)/shard_map/pack_columns/pallas_call | solution.py:507
  18.2 6.1 %collective-permute-start.3 = (f32[40,512]{1,0:T(8,128)S(1)}, f32[40,512]{1,0:T(8,128)S(1)}, u32[]{:S(2)}, u32[]{:S(2)}) collective-permute-start(f32[40,512]{1,0:T(8,128)S(1)} %pack_columns.1), channel_id=1, source_target_pairs={{1,0},{2,1},{3,2},{5,4},{6,5},{7,6},{9,8},{10,9},{11,10},{13,12},{... | collective-permute-start | bytes 245768 | tf_op jit(solution)/shard_map/ppermute | solution.py:461
  24.3 1.9 %collective-permute-start.2 = (f32[40,512]{1,0:T(8,128)S(1)}, f32[40,512]{1,0:T(8,128)S(1)}, u32[]{:S(2)}, u32[]{:S(2)}) collective-permute-start(f32[40,512]{1,0:T(8,128)S(1)} %pack_columns.1), channel_id=1, source_target_pairs={{0,1},{1,2},{2,3},{4,5},{5,6},{6,7},{8,9},{9,10},{10,11},{12,13},{... | collective-permute-start | bytes 245768 | tf_op jit(solution)/shard_map/ppermute | solution.py:461
  26.2 2.8 %near_residual.1.near = f32[9,8,32,256]{3,2,1,0:T(8,128)S(1)} custom-call(f32[5,32,256]{2,1,0:T(8,128)S(1)} %collective-permute-done.above, f32[5,32,256]{2,1,0:T(8,128)S(1)} %collective-permute-done.1.below, f32[8,32,256]{2,1,0:T(8,128)S(1)} %copy-done, f32[8,32,256]{2,1,0:T(8,128)S(1)} %copy-done.1, f32[8,32,256]{2,1,0:T(8,128)S(1)} %copy-done.2, ...), custom_call_target="tpu_custom_call" | custom-call | flops 9830400 | bytes 8126464 | tf_op jit(solution)/shard_map/near_residual/pallas_call | solution.py:520
  29.0 0.0 collective-permute-done.3.right
  29.0 1.6 %collective-permute-done.2.left = f32[40,512]{1,0:T(8,128)S(1)} collective-permute-done((f32[40,512]{1,0:T(8,128)S(1)}, f32[40,512]{1,0:T(8,128)S(1)}, u32[]{:S(2)}, u32[]{:S(2)}) %collective-permute-start.2) | collective-permute-done | bytes 81952 | tf_op jit(solution)/shard_map/ppermute | solution.py:461
  30.6 4.6 %finish.1 = (f32[9,8,32,256]{3,2,1,0:T(8,128)}, f32[8,32,256]{2,1,0:T(8,128)}) custom-call(f32[40,512]{1,0:T(8,128)S(1)} %collective-permute-done.2.left, f32[40,512]{1,0:T(8,128)S(1)} %collective-permute-done.3.right, f32[5,32,256]{2,1,0:T(8,128)S(1)} %collective-permute-done.above, f32[5,32,256]{2,1,0:T(8,128)S(1)} %collective-permute-done.1.below, ...), custom_call_target="tpu_custom_call" | custom-call | tf_op jit(solution)/shard_map/finish/pallas_call | solution.py:534
  (3 shorter events, 0.0 us)
Async XLA Ops:
  0.6 12.2 %copy-start = (f32[8,32,256]{2,1,0:T(8,128)S(1)}, f32[8,32,256]{2,1,0:T(8,128)}, u32[]{:S(2)}) copy-start(f32[8,32,256]{2,1,0:T(8,128)} %press.9) | copy-start | bytes 786436
  0.6 12.2 %copy-start.4 = (f32[8,32,256]{2,1,0:T(8,128)S(1)}, f32[8,32,256]{2,1,0:T(8,128)}, u32[]{:S(2)}) copy-start(f32[8,32,256]{2,1,0:T(8,128)} %pore.7) | copy-start | bytes 786436
  0.7 12.2 %copy-start.8 = (s32[4,8]{1,0:T(4,128)S(1)}, s32[4,8]{1,0:T(4,128)}, u32[]{:S(2)}) copy-start(s32[4,8]{1,0:T(4,128)} %flags.3) | copy-start | bytes 388
  0.7 12.2 %copy-start.7 = (f32[9,9]{1,0:T(8,128)S(1)}, f32[9,9]{1,0:T(8,128)}, u32[]{:S(2)}) copy-start(f32[9,9]{1,0:T(8,128)} %mix.3) | copy-start | bytes 976
  0.7 12.2 %copy-start.10 = (f32[9]{0:T(128)S(1)}, f32[9]{0:T(128)}, u32[]{:S(2)}) copy-start(f32[9]{0:T(128)} %slope.3) | copy-start | bytes 112
  0.7 12.2 %copy-start.9 = (f32[9]{0:T(128)S(1)}, f32[9]{0:T(128)}, u32[]{:S(2)}) copy-start(f32[9]{0:T(128)} %vol.3) | copy-start | bytes 112
  0.7 12.2 %copy-start.6 = (f32[9,8,32,256]{3,2,1,0:T(8,128)S(1)}, f32[9,8,32,256]{3,2,1,0:T(8,128)}, u32[]{:S(2)}) copy-start(f32[9,8,32,256]{3,2,1,0:T(8,128)} %mass.3) | copy-start | bytes 7077892
  0.7 12.2 %copy-start.5 = (f32[9,8,32,256]{3,2,1,0:T(8,128)S(1)}, f32[9,8,32,256]{3,2,1,0:T(8,128)}, u32[]{:S(2)}) copy-start(f32[9,8,32,256]{3,2,1,0:T(8,128)} %comp.3) | copy-start | bytes 7077892
  6.4 10.7 %collective-permute-start = (f32[5,32,256]{2,1,0:T(8,128)S(1)}, f32[5,32,256]{2,1,0:T(8,128)S(1)}, u32[]{:S(2)}, u32[]{:S(2)}) collective-permute-start(f32[5,32,256]{2,1,0:T(8,128)S(1)} %get-tuple-element.12), channel_id=1, source_target_pairs={{0,4},{4,8},{8,12},{12,16},{16,20},{20,24},{24,28},{1,5},{5,9},{9,... | collective-permute-start | bytes 491528 | tf_op jit(solution)/shard_map/ppermute | solution.py:461
  8.3 8.8 %collective-permute-start.1 = (f32[5,32,256]{2,1,0:T(8,128)S(1)}, f32[5,32,256]{2,1,0:T(8,128)S(1)}, u32[]{:S(2)}, u32[]{:S(2)}) collective-permute-start(f32[5,32,256]{2,1,0:T(8,128)S(1)} %get-tuple-element.13), channel_id=1, source_target_pairs={{4,0},{8,4},{12,8},{16,12},{20,16},{24,20},{28,24},{5,1},{9,5},{13... | collective-permute-start | bytes 491528 | tf_op jit(solution)/shard_map/ppermute | solution.py:461
  12.9 4.2 %copy-start.1 = (f32[8,32,256]{2,1,0:T(8,128)S(1)}, f32[8,32,256]{2,1,0:T(8,128)}, u32[]{:S(2)}) copy-start(f32[8,32,256]{2,1,0:T(8,128)} %tx.5) | copy-start | bytes 786436
  12.9 4.2 %copy-start.2 = (f32[8,32,256]{2,1,0:T(8,128)S(1)}, f32[8,32,256]{2,1,0:T(8,128)}, u32[]{:S(2)}) copy-start(f32[8,32,256]{2,1,0:T(8,128)} %ty.5) | copy-start | bytes 786436
  12.9 4.2 %copy-start.3 = (f32[8,32,256]{2,1,0:T(8,128)S(1)}, f32[8,32,256]{2,1,0:T(8,128)}, u32[]{:S(2)}) copy-start(f32[8,32,256]{2,1,0:T(8,128)} %tz.5) | copy-start | bytes 786436
  18.2 10.8 %collective-permute-start.3 = (f32[40,512]{1,0:T(8,128)S(1)}, f32[40,512]{1,0:T(8,128)S(1)}, u32[]{:S(2)}, u32[]{:S(2)}) collective-permute-start(f32[40,512]{1,0:T(8,128)S(1)} %pack_columns.1), channel_id=1, source_target_pairs={{1,0},{2,1},{3,2},{5,4},{6,5},{7,6},{9,8},{10,9},{11,10},{13,12},{... | collective-permute-start | bytes 245768 | tf_op jit(solution)/shard_map/ppermute | solution.py:461
  24.3 6.3 %collective-permute-start.2 = (f32[40,512]{1,0:T(8,128)S(1)}, f32[40,512]{1,0:T(8,128)S(1)}, u32[]{:S(2)}, u32[]{:S(2)}) collective-permute-start(f32[40,512]{1,0:T(8,128)S(1)} %pack_columns.1), channel_id=1, source_target_pairs={{0,1},{1,2},{2,3},{4,5},{5,6},{6,7},{8,9},{9,10},{10,11},{12,13},{... | collective-permute-start | bytes 245768 | tf_op jit(solution)/shard_map/ppermute | solution.py:461

commit v3 on v2

--- a/solution.py
+++ b/solution.py
@@ -149,11 +149,11 @@
                 )
 
 
-def row_tiles(above, below, wanted):
+def row_tiles(above, below, wanted, start=0, stop=None):
     shape = above.shape[1:]
     upper = row_of(shape) % DEPTH_SLOTS < 2
     tile_row = row_of((ROWS, shape[1]))
-    depth = shape[0] // DEPTH_SLOTS
+    stop = stop or shape[0] // DEPTH_SLOTS
     tiles = {}
     for n, unit in enumerate(UNITS):
         fields = unit if isinstance(unit, tuple) else (unit,)
@@ -163,7 +163,7 @@
         if n % 2:
             up, down = pltpu.roll(up, shape[0] - 2, 0), pltpu.roll(down, 2, 0)
         both = jnp.where(upper, up, down)
-        for z in range(depth):
+        for z in range(start, stop):
             at = (z // 2) * ROWS
             tile = pltpu.roll(both[at : at + ROWS], 6 - 4 * (z % 2), 0)
             if fields[0] in wanted:
@@ -220,21 +220,23 @@
     return fields
 
 
-def own_cells(pack, flags, vol, slope, mix, comp, press, pore, mass, *rest):
+def own_cells(edge, start, flags, vol, slope, mix, comp, press, pore, mass, *rest):
     per_tile = 2
-    if pack:
+    if edge:
         tx, ty, tz, mob_ref, acc_ref, mob_sum, acc_sum, low_ref, high_ref, operand = rest
         tile_row = pl.program_id(0) * (flags.shape[1] // per_tile - 1)
+
+        @pl.when((pl.program_id(0) == 0) & (pl.program_id(1) == 0))
+        def _():
+            operand[...] = mixing_operand(mix)
+
     else:
-        mob_ref, acc_ref, mob_sum, acc_sum, operand = rest[-5:]
-        tile_row = pl.program_id(0) + 1
+        mob_ref, acc_ref, mob_sum, acc_sum = rest[-4:]
+        operand = mix
+        tile_row = pl.program_id(0) + start
     layer = lax.axis_index("layer")
     signed, slopes = parameters(vol, slope)
     planes, _, width = press.shape
-
-    @pl.when((pl.program_id(0) == 0) & (pl.program_id(1) == 0))
-    def _():
-        operand[...] = mixing_operand(mix)
 
     raw = [comp[i] for i in range(COMPS)]
     inverse = rcp(total_of(raw))
@@ -269,7 +271,7 @@
             mob_ref[i] = feed[i]
         mob_sum[...] = total_of(feed)
 
-    if not pack:
+    if not edge:
         return
     rest_fields = {
         MOB: mob_sum, PRESS: press, TX: tx, TY: ty, TZ: tz, PORE: pore, ACC: acc_sum,
@@ -288,7 +290,8 @@
         pack_rows(field, None, high_ref, planes)
 
 
-def near_residual(above, below, press, tx, ty, tz, mob, acc, out_ref, rows_h, press_h, tx_h):
+def near_residual(start, count, above, below, press, tx, ty, tz, mob, acc, *rest):
+    out_ref, rows_h, press_h, tx_h = rest[-4:]
     step = pl.program_id(0)
     planes = out_ref.shape[1]
     depth, rows, width = press.shape
@@ -297,23 +300,24 @@
 
     @pl.when(step == 0)
     def _():
-        tiles = row_tiles(above, below, (PRESS, TX, *range(COMPS)))
-        for z in range(depth):
-            press_h[z] = tiles[PRESS][z]
-            tx_h[z] = tiles[TX][z]
+        tiles = row_tiles(above, below, (PRESS, TX, *range(COMPS)), start, start + count)
+        for n in range(count):
+            press_h[n] = tiles[PRESS][n]
+            tx_h[n] = tiles[TX][n]
             for i in range(COMPS):
-                rows_h[i, z] = tiles[i][z]
+                rows_h[i, n] = tiles[i][n]
 
     own = slice(0, rows)
     scale = 0.5 * TIME_STEP
     end_x = (row_of((tall, width)) == rows - 1) & (areal == areals - 1)
     end_y = lane_of((rows, width)) == width - 1
     for plane in range(planes):
-        z = step * planes + plane
+        n = step * planes + plane
+        z = start + n
         down, up = jnp.maximum(z - 1, 0), jnp.minimum(z + 1, depth - 1)
         p = press[z]
-        p_tall = jnp.concatenate([p, press_h[z]], axis=0)
-        t_tall = jnp.where(end_x, 0.0, scale * jnp.concatenate([tx[z], tx_h[z]], axis=0))
+        p_tall = jnp.concatenate([p, press_h[n]], axis=0)
+        t_tall = jnp.where(end_x, 0.0, scale * jnp.concatenate([tx[z], tx_h[n]], axis=0))
         gx = t_tall * (p_tall - pltpu.roll(p_tall, tall - 1, 0))
         gx_low = -pltpu.roll(gx, 1, 0)[own]
         gx = gx[own]
@@ -324,7 +328,7 @@
         middle = (gx + gx_low) + (gy + gy_low) + (gz + gz_low)
         for i in range(COMPS):
             here = mob[i, z]
-            tall_here = jnp.concatenate([here, rows_h[i, z]], axis=0)
+            tall_here = jnp.concatenate([here, rows_h[i, n]], axis=0)
             out_ref[i, plane] = (
                 acc[i, z]
                 + middle * here
@@ -471,38 +475,42 @@
     def pinned(x):
         return pltpu.with_memory_space_constraint(x, pltpu.HBM)
 
-    def own(pack, before):
-        tile_row = (lambda g: g * (tiles - 1)) if pack else (lambda g: g + 1)
-        plane = pl.BlockSpec((PLANES, ROWS, width), lambda g, z: (z, tile_row(g), 0))
-        planes = pl.BlockSpec((COMPS, PLANES, ROWS, width), lambda g, z: (0, z, tile_row(g), 0))
+    operand = jax.ShapeDtypeStruct((PART, DEEP), jnp.bfloat16)
+    anywhere = pl.BlockSpec(memory_space=pl.ANY)
+
+    def own(edge, start, count, small, before):
+        tile_row = (lambda t: t * (tiles - 1)) if edge else (lambda t: start + t)
+        plane = pl.BlockSpec((PLANES, ROWS, width), lambda t, z: (z, tile_row(t), 0))
+        planes = pl.BlockSpec((COMPS, PLANES, ROWS, width), lambda t, z: (0, z, tile_row(t), 0))
         block = (len(UNITS) // 2, DEPTH_SLOTS * PLANES, width)
-        low = pl.BlockSpec(block, lambda g, z: (0, jnp.where(g == 0, z, parts - 1), 0))
-        high = pl.BlockSpec(block, lambda g, z: (0, jnp.where(g == 0, 0, z), 0))
-        count = 2 if pack else tiles - 2
+        low = pl.BlockSpec(block, lambda t, z: (0, jnp.where(t == 0, z, parts - 1), 0))
+        high = pl.BlockSpec(block, lambda t, z: (0, jnp.where(t == 0, 0, z), 0))
         cells = count * ROWS * depth * width
+        used = fields if edge else fields[:4]
         return pl.pallas_call(
-            functools.partial(own_cells, pack),
+            functools.partial(own_cells, edge, start),
             grid=(count, parts),
-            in_specs=[smem] * 4
+            in_specs=[smem] * 3
+            + [smem if edge else vmem]
             + [planes, plane, plane, planes]
-            + [plane] * (3 if pack else 0)
-            + [pl.BlockSpec(memory_space=pl.ANY)] * len(before),
-            out_specs=[planes, planes, plane, plane] + ([low, high] if pack else []),
-            out_shape=[whole, whole, sums, sums] + ([packed, packed] if pack else []),
-            input_output_aliases={8 + k: k for k in range(len(before))},
-            scratch_shapes=[pltpu.VMEM((PART, DEEP), jnp.bfloat16)],
+            + [plane] * (len(used) - 4)
+            + [anywhere] * len(before),
+            out_specs=[planes, planes, plane, plane] + ([low, high, vmem] if edge else []),
+            out_shape=[whole, whole, sums, sums] + ([packed, packed, operand] if edge else []),
+            input_output_aliases={4 + len(used) + k: k for k in range(len(before))},
             compiler_params=params(24),
-            cost_estimate=pl.CostEstimate(
-                flops=900 * cells, transcendentals=190 * cells, bytes_accessed=4 * 39 * cells
-            ),
-            name="edge_cells" if pack else "inner_cells",
-        )(*(pinned(x) if pack else x for x in (*scalars, *fields[: None if pack else 4])), *before)
-
-    *begun, low, high = own(True, ())
-
+            cost_estimate=pl.CostEstimate(flops=cells, transcendentals=0, bytes_accessed=cells),
+            name="edge_cells" if edge else "inner_cells",
+        )(*(pinned(x) if edge else x for x in (*small, *used)), *before)
+
+    *begun, low, high, mixer = own(True, 0, 2, scalars, ())
+    small = (*scalars[:3], mixer)
+    early = (tiles - 2) // 2
+    below = moved(low, "areal", -1)
+    begun = own(False, 1, early, small, begun)
+    high, begun = lax.optimization_barrier((high, begun))
     above = moved(high, "areal", 1)
-    below = moved(low, "areal", -1)
-    mob, acc, mob_sum, acc_sum = own(False, begun)
+    mob, acc, mob_sum, acc_sum = own(False, 1 + early, tiles - 2 - early, small, begun)
 
     packet = pl.pallas_call(
         pack_columns,
@@ -512,22 +520,31 @@
         compiler_params=params(24),
         name="pack_columns",
     )(above, below, mob, mob_sum, pressure, trans_x, trans_y, trans_z, pore_volume, acc_sum)
+
+    def residual(start, count, before):
+        cells = rows * count * width
+        row_tile = pltpu.VMEM((count, ROWS, width), f32)
+        return pl.pallas_call(
+            functools.partial(near_residual, start, count),
+            grid=(count // 2,),
+            in_specs=[vmem] * 8 + [anywhere] * len(before),
+            out_specs=pl.BlockSpec((COMPS, 2, rows, width), lambda s: (0, s + start // 2, 0, 0)),
+            out_shape=whole,
+            input_output_aliases={8: 0} if before else {},
+            scratch_shapes=[pltpu.VMEM((COMPS, count, ROWS, width), f32), row_tile, row_tile],
+            compiler_params=params(24),
+            cost_estimate=pl.CostEstimate(
+                flops=150 * cells, transcendentals=0, bytes_accessed=4 * 31 * cells
+            ),
+            name="near_residual",
+        )(above, below, pressure, trans_x, trans_y, trans_z, mob, acc, *before)
+
     left = moved(packet, "layer", 1)
+    near = residual(0, depth // 2, ())
+    packet, near = lax.optimization_barrier((packet, near))
     right = moved(packet, "layer", -1)
+    near = residual(depth // 2, depth - depth // 2, (near,))
     planes = pl.BlockSpec((COMPS, 2, rows, width), lambda s: (0, s, 0, 0))
-    row_tile = pltpu.VMEM((depth, ROWS, width), f32)
-    cells = rows * depth * width
-    near = pl.pallas_call(
-        near_residual,
-        grid=(depth // 2,),
-        in_specs=[vmem] * 8,
-        out_specs=planes,
-        out_shape=whole,
-        scratch_shapes=[pltpu.VMEM((COMPS, depth, ROWS, width), f32), row_tile, row_tile],
-        compiler_params=params(24),
-        cost_estimate=pl.CostEstimate(flops=150 * cells, transcendentals=0, bytes_accessed=4 * 31 * cells),
-        name="near_residual",
-    )(above, below, pressure, trans_x, trans_y, trans_z, mob, acc)
 
     extended = pltpu.VMEM((depth, rows + ROWS, width + LANES), f32)
     side = pltpu.VMEM((depth, rows, LANES), f32)

time: 35.4 us -> 38.9 us (1.099); the launches traced: 35.2 us -> 38.2 us
  waiting for transfers between devices: 1.61 us -> 4.38 us
  Pallas kernels: 18.2 us -> 20.8 us
  starting transfers between devices: 14.4 us -> 12.2 us
    ppermute x4, waiting for transfers between devices: 1.61 us -> 4.38 us  [moved(): return lax.ppermute(block, axis, pairs)]
    pallas_call x3 -> x5, Pallas kernels: 12.5 us -> 15.1 us  [the longest x3 12.2 us: own(): pl.pallas_call(functools.partial(own_cells, edge, start), grid=(count, pa...]
    ppermute x4, starting transfers between devices: 14.4 us -> 12.2 us  [moved(): return lax.ppermute(block, axis, pairs)]
  transfers between devices with their start and end apart: 4 -> 4, of which waited for: 1 -> 2; matrix products, arithmetic and copies ran while one was open for 0% -> 0% of each run, Pallas kernels for 20% -> 25%
where the time goes in v3:
time: 38.9 us; the launch traced here: 38.2 us
  Pallas kernels  20.8 us (53%)
  starting transfers between devices  12.2 us (31%)
  waiting for transfers between devices  4.38 us (11%)
  between operations  0.87 us (2%)
    pallas_call x3, Pallas kernels, own(): pl.pallas_call(functools.partial(own_cells, edge, start), grid=(count, pa...  12.2 us
    ppermute x4, starting transfers between devices, moved(): return lax.ppermute(block, axis, pairs)  12.2 us
    pallas_call x1, Pallas kernels, on_device(): pl.pallas_call(finish, grid=(depth // 2,), in_specs=[vmem] * 12 + [planes...  4.64 us
    ppermute x4, waiting for transfers between devices, moved(): return lax.ppermute(block, axis, pairs)  4.38 us
    pallas_call x2, Pallas kernels, residual(): pl.pallas_call(functools.partial(near_residual, start, count), grid=(coun...  2.86 us
    pallas_call x1, Pallas kernels, on_device(): pl.pallas_call(pack_columns, in_specs=[vmem] * 10, out_specs=vmem, out_sh...  1.06 us
  transfers between devices with their start and end apart: 4, of which 2 were waited for; matrix products, arithmetic and copies ran while one was open for 0% of the time, Pallas kernels for 25%

profile of v3, /device:TPU:12, one launch (start us, length us, event | category | flops | bytes accessed | tf_op | source)
XLA Modules:
  0.0 38.2 jit_solution(9372067581532773290)
XLA Ops:
  0.6 0.0 copy-start.2
  0.6 0.0 copy-start.6
  0.7 0.0 copy-start.7
  0.7 0.0 copy-start.9
  0.7 0.0 copy-start.8
  0.7 0.0 copy-start.1
  0.7 0.0 copy-start
  0.7 5.6 %edge_cells.1 = (f32[9,8,32,256]{3,2,1,0:T(8,128)S(1)}, f32[9,8,32,256]{3,2,1,0:T(8,128)S(1)}, f32[8,32,256]{2,1,0:T(8,128)S(1)}, f32[8,32,256]{2,1,0:T(8,128)S(...) custom-call(s32[4,8]{1,0:T(4,128)} %flags.5, f32[9]{0:T(128)} %vol.5, ...), custom_call_target="tpu_custom_call" | custom-call | flops 32768 | bytes 32768 | tf_op jit(solution)/shard_map/edge_cells/pallas_call | solution.py:490
  6.3 4.3 %collective-permute-start.1 = (f32[5,32,256]{2,1,0:T(8,128)S(1)}, f32[5,32,256]{2,1,0:T(8,128)S(1)}, u32[]{:S(2)}, u32[]{:S(2)}) collective-permute-start(f32[5,32,256]{2,1,0:T(8,128)S(1)} %get-tuple-element.35), channel_id=1, source_target_pairs={{4,0},{8,4},{12,8},{16,12},{20,16},{24,20},{28,24},{5,1},{9,5},{13... | collective-permute-start | bytes 491528 | tf_op jit(solution)/shard_map/ppermute | solution.py:465
  10.6 0.0 copy-done.2
  10.6 0.0 copy-done.6
  10.6 0.0 copy-done.7
  10.6 0.0 copy-done.9
  10.6 0.0 copy-done.8
  10.6 0.0 copy-done.1
  10.7 3.3 %inner_cells.2 = (f32[9,8,32,256]{3,2,1,0:T(8,128)S(1)}, f32[9,8,32,256]{3,2,1,0:T(8,128)S(1)}, f32[8,32,256]{2,1,0:T(8,128)S(1)}, f32[8,32,256]{2,1,0:T(8,128)S(1)}) custom-call(s32[4,8]{1,0:T(4,128)S(1)} %copy-done.7, f32[9]{0:T(128)S(1)} %copy-done.8, f32[9]{0:T(128)S(1)} %copy-done.9, ...), custom_call_target="tpu_custom_call", output_to_operand_aliasing={{0}: (8, {}), {1}: (9, {}), {2}: (10, {}), {3}: (11, {})} | custom-call | flops 16384 | bytes 16384 | tf_op jit(solution)/shard_map/inner_cells/pallas_call | solution.py:490
  14.0 0.0 copy-start.3
  14.0 0.0 copy-start.4
  14.0 0.0 copy-start.5
  14.0 2.1 %collective-permute-start = (f32[5,32,256]{2,1,0:T(8,128)S(1)}, f32[5,32,256]{2,1,0:T(8,128)S(1)}, u32[]{:S(2)}, u32[]{:S(2)}) collective-permute-start(f32[5,32,256]{2,1,0:T(8,128)S(1)} %get-tuple-element.34), channel_id=1, source_target_pairs={{0,4},{4,8},{8,12},{12,16},{16,20},{20,24},{24,28},{1,5},{5,9},{9,... | collective-permute-start | bytes 491528 | tf_op jit(solution)/shard_map/ppermute | solution.py:465
  16.1 3.3 %inner_cells.3 = (f32[9,8,32,256]{3,2,1,0:T(8,128)S(1)}, f32[9,8,32,256]{3,2,1,0:T(8,128)S(1)}, f32[8,32,256]{2,1,0:T(8,128)S(1)}, f32[8,32,256]{2,1,0:T(8,128)S(1)}) custom-call(s32[4,8]{1,0:T(4,128)S(1)} %copy-done.7, f32[9]{0:T(128)S(1)} %copy-done.8, f32[9]{0:T(128)S(1)} %copy-done.9, ...), custom_call_target="tpu_custom_call", output_to_operand_aliasing={{0}: (8, {}), {1}: (9, {}), {2}: (10, {}), {3}: (11, {})} | custom-call | flops 16384 | bytes 16384 | tf_op jit(solution)/shard_map/inner_cells/pallas_call | solution.py:490
  19.4 0.0 collective-permute-done.1.below
  19.4 2.3 %collective-permute-done.above = f32[5,32,256]{2,1,0:T(8,128)S(1)} collective-permute-done((f32[5,32,256]{2,1,0:T(8,128)S(1)}, f32[5,32,256]{2,1,0:T(8,128)S(1)}, u32[]{:S(2)}, u32[]{:S(2)}) %collective-permute-start) | collective-permute-done | bytes 163872 | tf_op jit(solution)/shard_map/ppermute | solution.py:465
  21.7 0.0 copy-done.4
  21.7 1.1 %pack_columns.1 = f32[40,512]{1,0:T(8,128)S(1)} custom-call(f32[5,32,256]{2,1,0:T(8,128)S(1)} %collective-permute-done.above, f32[5,32,256]{2,1,0:T(8,128)S(1)} %collective-permute-done.1.below, f32[9,8,32,256]{3,2,1,0:T(8,128)S(1)} %get-tuple-element.40.mob, f32[8,32,256]{2,1,0:T(8,128)S(1)} %get-tuple-element.41.mob_sum, f32[8,32,256]{2,1,0:T(8,128)S(1)} %copy-done.2, ...), custom_call_target="tpu_custom_call" | custom-call | tf_op jit(solution)/shard_map/pack_columns/pallas_call | solution.py:515
  22.7 1.9 %collective-permute-start.2 = (f32[40,512]{1,0:T(8,128)S(1)}, f32[40,512]{1,0:T(8,128)S(1)}, u32[]{:S(2)}, u32[]{:S(2)}) collective-permute-start(f32[40,512]{1,0:T(8,128)S(1)} %pack_columns.1), channel_id=1, source_target_pairs={{0,1},{1,2},{2,3},{4,5},{5,6},{6,7},{8,9},{9,10},{10,11},{12,13},{... | collective-permute-start | bytes 245768 | tf_op jit(solution)/shard_map/ppermute | solution.py:465
  24.7 1.4 %near_residual.2.rest_0_ = f32[9,8,32,256]{3,2,1,0:T(8,128)S(1)} custom-call(f32[5,32,256]{2,1,0:T(8,128)S(1)} %collective-permute-done.above, f32[5,32,256]{2,1,0:T(8,128)S(1)} %collective-permute-done.1.below, f32[8,32,256]{2,1,0:T(8,128)S(1)} %copy-done.2, f32[8,32,256]{2,1,0:T(8,128)S(1)} %copy-done.3, f32[8,32,256]{2,1,0:T(8,128)S(1)} %copy-done.4, ...), custom_call_target="tpu_custom_call" | custom-call | flops 4915200 | bytes 4063232 | tf_op jit(solution)/shard_map/near_residual/pallas_call | solution.py:527
  26.1 3.9 %collective-permute-start.3 = (f32[40,512]{1,0:T(8,128)S(1)}, f32[40,512]{1,0:T(8,128)S(1)}, u32[]{:S(2)}, u32[]{:S(2)}) collective-permute-start(f32[40,512]{1,0:T(8,128)S(1)} %pack_columns.1), channel_id=1, source_target_pairs={{1,0},{2,1},{3,2},{5,4},{6,5},{7,6},{9,8},{10,9},{11,10},{13,12},{... | collective-permute-start | bytes 245768 | tf_op jit(solution)/shard_map/ppermute | solution.py:465
  30.0 1.4 %near_residual.3.near = f32[9,8,32,256]{3,2,1,0:T(8,128)S(1)} custom-call(f32[5,32,256]{2,1,0:T(8,128)S(1)} %collective-permute-done.above, f32[5,32,256]{2,1,0:T(8,128)S(1)} %collective-permute-done.1.below, f32[8,32,256]{2,1,0:T(8,128)S(1)} %copy-done.2, f32[8,32,256]{2,1,0:T(8,128)S(1)} %copy-done.3, ...), custom_call_target="tpu_custom_call", output_to_operand_aliasing={{}: (8, {})} | custom-call | flops 4915200 | bytes 4063232 | tf_op jit(solution)/shard_map/near_residual/pallas_call | solution.py:527
  31.5 0.0 collective-permute-done.2.left
  31.5 2.1 %collective-permute-done.3.right = f32[40,512]{1,0:T(8,128)S(1)} collective-permute-done((f32[40,512]{1,0:T(8,128)S(1)}, f32[40,512]{1,0:T(8,128)S(1)}, u32[]{:S(2)}, u32[]{:S(2)}) %collective-permute-start.3) | collective-permute-done | bytes 81952 | tf_op jit(solution)/shard_map/ppermute | solution.py:465
  33.6 4.6 %finish.1 = (f32[9,8,32,256]{3,2,1,0:T(8,128)}, f32[8,32,256]{2,1,0:T(8,128)}) custom-call(f32[40,512]{1,0:T(8,128)S(1)} %collective-permute-done.2.left, f32[40,512]{1,0:T(8,128)S(1)} %collective-permute-done.3.right, f32[5,32,256]{2,1,0:T(8,128)S(1)} %collective-permute-done.above, f32[5,32,256]{2,1,0:T(8,128)S(1)} %collective-permute-done.1.below, ...), custom_call_target="tpu_custom_call" | custom-call | tf_op jit(solution)/shard_map/finish/pallas_call | solution.py:551
  (3 shorter events, 0.0 us)
Async XLA Ops:
  0.6 10.0 %copy-start.2 = (f32[8,32,256]{2,1,0:T(8,128)S(1)}, f32[8,32,256]{2,1,0:T(8,128)}, u32[]{:S(2)}) copy-start(f32[8,32,256]{2,1,0:T(8,128)} %press.13) | copy-start | bytes 786436
  0.6 10.0 %copy-start.6 = (f32[8,32,256]{2,1,0:T(8,128)S(1)}, f32[8,32,256]{2,1,0:T(8,128)}, u32[]{:S(2)}) copy-start(f32[8,32,256]{2,1,0:T(8,128)} %pore.9) | copy-start | bytes 786436
  0.7 10.0 %copy-start.7 = (s32[4,8]{1,0:T(4,128)S(1)}, s32[4,8]{1,0:T(4,128)}, u32[]{:S(2)}) copy-start(s32[4,8]{1,0:T(4,128)} %flags.5) | copy-start | bytes 388
  0.7 10.0 %copy-start.9 = (f32[9]{0:T(128)S(1)}, f32[9]{0:T(128)}, u32[]{:S(2)}) copy-start(f32[9]{0:T(128)} %slope.5) | copy-start | bytes 112
  0.7 10.0 %copy-start.8 = (f32[9]{0:T(128)S(1)}, f32[9]{0:T(128)}, u32[]{:S(2)}) copy-start(f32[9]{0:T(128)} %vol.5) | copy-start | bytes 112
  0.7 10.0 %copy-start.1 = (f32[9,8,32,256]{3,2,1,0:T(8,128)S(1)}, f32[9,8,32,256]{3,2,1,0:T(8,128)}, u32[]{:S(2)}) copy-start(f32[9,8,32,256]{3,2,1,0:T(8,128)} %mass.5) | copy-start | bytes 7077892
  0.7 10.0 %copy-start = (f32[9,8,32,256]{3,2,1,0:T(8,128)S(1)}, f32[9,8,32,256]{3,2,1,0:T(8,128)}, u32[]{:S(2)}) copy-start(f32[9,8,32,256]{3,2,1,0:T(8,128)} %comp.5) | copy-start | bytes 7077892
  6.3 13.0 %collective-permute-start.1 = (f32[5,32,256]{2,1,0:T(8,128)S(1)}, f32[5,32,256]{2,1,0:T(8,128)S(1)}, u32[]{:S(2)}, u32[]{:S(2)}) collective-permute-start(f32[5,32,256]{2,1,0:T(8,128)S(1)} %get-tuple-element.35), channel_id=1, source_target_pairs={{4,0},{8,4},{12,8},{16,12},{20,16},{24,20},{28,24},{5,1},{9,5},{13... | collective-permute-start | bytes 491528 | tf_op jit(solution)/shard_map/ppermute | solution.py:465
  14.0 7.7 %copy-start.3 = (f32[8,32,256]{2,1,0:T(8,128)S(1)}, f32[8,32,256]{2,1,0:T(8,128)}, u32[]{:S(2)}) copy-start(f32[8,32,256]{2,1,0:T(8,128)} %tx.7) | copy-start | bytes 786436
  14.0 7.7 %copy-start.4 = (f32[8,32,256]{2,1,0:T(8,128)S(1)}, f32[8,32,256]{2,1,0:T(8,128)}, u32[]{:S(2)}) copy-start(f32[8,32,256]{2,1,0:T(8,128)} %ty.7) | copy-start | bytes 786436
  14.0 7.7 %copy-start.5 = (f32[8,32,256]{2,1,0:T(8,128)S(1)}, f32[8,32,256]{2,1,0:T(8,128)}, u32[]{:S(2)}) copy-start(f32[8,32,256]{2,1,0:T(8,128)} %tz.7) | copy-start | bytes 786436
  14.0 7.7 %collective-permute-start = (f32[5,32,256]{2,1,0:T(8,128)S(1)}, f32[5,32,256]{2,1,0:T(8,128)S(1)}, u32[]{:S(2)}, u32[]{:S(2)}) collective-permute-start(f32[5,32,256]{2,1,0:T(8,128)S(1)} %get-tuple-element.34), channel_id=1, source_target_pairs={{0,4},{4,8},{8,12},{12,16},{16,20},{20,24},{24,28},{1,5},{5,9},{9,... | collective-permute-start | bytes 491528 | tf_op jit(solution)/shard_map/ppermute | solution.py:465
  22.7 8.7 %collective-permute-start.2 = (f32[40,512]{1,0:T(8,128)S(1)}, f32[40,512]{1,0:T(8,128)S(1)}, u32[]{:S(2)}, u32[]{:S(2)}) collective-permute-start(f32[40,512]{1,0:T(8,128)S(1)} %pack_columns.1), channel_id=1, source_target_pairs={{0,1},{1,2},{2,3},{4,5},{5,6},{6,7},{8,9},{9,10},{10,11},{12,13},{... | collective-permute-start | bytes 245768 | tf_op jit(solution)/shard_map/ppermute | solution.py:465
  26.1 7.5 %collective-permute-start.3 = (f32[40,512]{1,0:T(8,128)S(1)}, f32[40,512]{1,0:T(8,128)S(1)}, u32[]{:S(2)}, u32[]{:S(2)}) collective-permute-start(f32[40,512]{1,0:T(8,128)S(1)} %pack_columns.1), channel_id=1, source_target_pairs={{1,0},{2,1},{3,2},{5,4},{6,5},{7,6},{9,8},{10,9},{11,10},{13,12},{... | collective-permute-start | bytes 245768 | tf_op jit(solution)/shard_map/ppermute | solution.py:465

commit v4 on v3

--- a/solution.py
+++ b/solution.py
@@ -149,8 +149,8 @@
                 )
 
 
-def row_tiles(above, below, wanted, start=0, stop=None):
-    shape = above.shape[1:]
+def row_tiles(one, two, wanted, start=0, stop=None):
+    shape = one.shape[1:]
     upper = row_of(shape) % DEPTH_SLOTS < 2
     tile_row = row_of((ROWS, shape[1]))
     stop = stop or shape[0] // DEPTH_SLOTS
@@ -159,7 +159,7 @@
         fields = unit if isinstance(unit, tuple) else (unit,)
         if not any(k in wanted for k in fields):
             continue
-        up, down = above[n // 2], below[n // 2]
+        up, down = by_side("areal", one[n // 2], two[n // 2])
         if n % 2:
             up, down = pltpu.roll(up, shape[0] - 2, 0), pltpu.roll(down, 2, 0)
         both = jnp.where(upper, up, down)
@@ -174,13 +174,13 @@
     return tiles
 
 
-def pack_columns(above, below, mob, mob_sum, press, tx, ty, tz, pore, acc_sum, out_ref):
+def pack_columns(rows_one, rows_two, mob, mob_sum, press, tx, ty, tz, pore, acc_sum, out_ref):
     depth, rows, width = press.shape
     shape = (rows + ROWS, LANES)
     lane = lane_of(shape)
     corner_fields = {MOB: mob_sum, PRESS: press, TX: tx, TY: ty}
     others = {TZ: tz, PORE: pore, ACC: acc_sum, **corner_fields}
-    corners = row_tiles(above, below, corner_fields)
+    corners = row_tiles(rows_one, rows_two, corner_fields)
     nothing = jnp.zeros((ROWS, LANES), jnp.float32)
     for tile in range(FIELDS // 4):
         packed = jnp.zeros(shape, jnp.float32)
@@ -205,17 +205,17 @@
         out_ref[:, tile * LANES : (tile + 1) * LANES] = packed
 
 
-def side_fields(left, right):
+def side_fields(one, two):
     fields = []
-    lane = lane_of((left.shape[0], LANES))
+    lane = lane_of((one.shape[0], LANES))
     for tile in range(FIELDS // 4):
         span = slice(tile * LANES, (tile + 1) * LANES)
-        l, r = left[:, span], right[:, span]
-        one = jnp.where(lane % 4 < 2, r, l)
+        l, r = by_side("layer", one[:, span], two[:, span])
+        mobility = jnp.where(lane % 4 < 2, r, l)
         other = jnp.where(lane % 4 < 2, l, r)
         for quarter in range(4):
             turn = (LANES - 32 * quarter) % LANES
-            both = one if 4 * tile + quarter < COMPS else other
+            both = mobility if 4 * tile + quarter < COMPS else other
             fields.append(pltpu.roll(both, turn, 1) if turn else both)
     return fields
 
@@ -223,7 +223,7 @@
 def own_cells(edge, start, flags, vol, slope, mix, comp, press, pore, mass, *rest):
     per_tile = 2
     if edge:
-        tx, ty, tz, mob_ref, acc_ref, mob_sum, acc_sum, low_ref, high_ref, operand = rest
+        tx, ty, tz, mob_ref, acc_ref, mob_sum, acc_sum, one_ref, two_ref, operand = rest
         tile_row = pl.program_id(0) * (flags.shape[1] // per_tile - 1)
 
         @pl.when((pl.program_id(0) == 0) & (pl.program_id(1) == 0))
@@ -281,16 +281,23 @@
         here = mob_ref[k, z] if k < COMPS else rest_fields[k][z]
         return here, here
 
-    @pl.when(pl.program_id(0) == 0)
-    def _():
-        pack_rows(field, low_ref, None, planes)
-
-    @pl.when(pl.program_id(0) == 1)
-    def _():
-        pack_rows(field, None, high_ref, planes)
-
-
-def near_residual(start, count, above, below, press, tx, ty, tz, mob, acc, *rest):
+    count = DEPTH_SLOTS * planes
+    at = pl.multiple_of(pl.program_id(1) * count, count)
+    odd = lax.axis_index("areal") % 2
+    for end in range(2):
+        for turn, ref in enumerate((one_ref, two_ref)):
+            @pl.when((pl.program_id(0) == end) & ((odd == 1) == (end == turn)))
+            def _():
+                here = ref.at[:, pl.ds(at, count), :]
+                pack_rows(field, *((here, None) if end == 0 else (None, here)), planes)
+
+
+def by_side(axis, one, two):
+    odd = lax.axis_index(axis) % 2 == 1
+    return jnp.where(odd, one, two), jnp.where(odd, two, one)
+
+
+def near_residual(start, count, rows_one, rows_two, press, tx, ty, tz, mob, acc, *rest):
     out_ref, rows_h, press_h, tx_h = rest[-4:]
     step = pl.program_id(0)
     planes = out_ref.shape[1]
@@ -300,7 +307,7 @@
 
     @pl.when(step == 0)
     def _():
-        tiles = row_tiles(above, below, (PRESS, TX, *range(COMPS)), start, start + count)
+        tiles = row_tiles(rows_one, rows_two, (PRESS, TX, *range(COMPS)), start, start + count)
         for n in range(count):
             press_h[n] = tiles[PRESS][n]
             tx_h[n] = tiles[TX][n]
@@ -342,7 +349,7 @@
 
 
 def finish(
-    left, right, above, below,
+    columns_one, columns_two, rows_one, rows_two,
     press, tx, ty, tz, pore, mob_sum, acc_sum, mob, near,
     res_ref, new_ref,
     side_h, e_press, e_tx, e_ty, e_tz, e_pore, e_mob, e_acc,
@@ -363,8 +370,8 @@
             MOB: (e_mob, mob_sum), PRESS: (e_press, press), TX: (e_tx, tx), TY: (e_ty, ty),
             TZ: (e_tz, tz), PORE: (e_pore, pore), ACC: (e_acc, acc_sum),
         }
-        tiles = row_tiles(above, below, extended)
-        columns = side_fields(left, right)
+        tiles = row_tiles(rows_one, rows_two, extended)
+        columns = side_fields(columns_one, columns_two)
         for i in range(COMPS):
             side_h[i] = columns[i][:rows]
         for k, (e_ref, own_ref) in extended.items():
@@ -459,10 +466,10 @@
 
     scalars = (two_phase, volatility, pressure_slope, mixing)
 
-    def moved(block, axis, shift):
+    def swapped(block, axis, first):
         count = lax.axis_size(axis)
-        pairs = [(i, i + shift) for i in range(count) if 0 <= i + shift < count]
-        return lax.ppermute(block, axis, pairs)
+        pairs = [(i, i + 1) for i in range(first, count - 1, 2)]
+        return lax.ppermute(block, axis, pairs + [(j, i) for i, j in pairs])
 
     whole = jax.ShapeDtypeStruct((COMPS, depth, rows, width), f32)
     sums = jax.ShapeDtypeStruct((depth, rows, width), f32)
@@ -482,9 +489,6 @@
         tile_row = (lambda t: t * (tiles - 1)) if edge else (lambda t: start + t)
         plane = pl.BlockSpec((PLANES, ROWS, width), lambda t, z: (z, tile_row(t), 0))
         planes = pl.BlockSpec((COMPS, PLANES, ROWS, width), lambda t, z: (0, z, tile_row(t), 0))
-        block = (len(UNITS) // 2, DEPTH_SLOTS * PLANES, width)
-        low = pl.BlockSpec(block, lambda t, z: (0, jnp.where(t == 0, z, parts - 1), 0))
-        high = pl.BlockSpec(block, lambda t, z: (0, jnp.where(t == 0, 0, z), 0))
         cells = count * ROWS * depth * width
         used = fields if edge else fields[:4]
         return pl.pallas_call(
@@ -495,22 +499,20 @@
             + [planes, plane, plane, planes]
             + [plane] * (len(used) - 4)
             + [anywhere] * len(before),
-            out_specs=[planes, planes, plane, plane] + ([low, high, vmem] if edge else []),
+            out_specs=[planes, planes, plane, plane] + ([vmem] * 3 if edge else []),
             out_shape=[whole, whole, sums, sums] + ([packed, packed, operand] if edge else []),
             input_output_aliases={4 + len(used) + k: k for k in range(len(before))},
             compiler_params=params(24),
-            cost_estimate=pl.CostEstimate(flops=cells, transcendentals=0, bytes_accessed=cells),
+            cost_estimate=pl.CostEstimate(
+                flops=900 * cells, transcendentals=190 * cells, bytes_accessed=4 * 39 * cells
+            ),
             name="edge_cells" if edge else "inner_cells",
         )(*(pinned(x) if edge else x for x in (*small, *used)), *before)
 
-    *begun, low, high, mixer = own(True, 0, 2, scalars, ())
-    small = (*scalars[:3], mixer)
-    early = (tiles - 2) // 2
-    below = moved(low, "areal", -1)
-    begun = own(False, 1, early, small, begun)
-    high, begun = lax.optimization_barrier((high, begun))
-    above = moved(high, "areal", 1)
-    mob, acc, mob_sum, acc_sum = own(False, 1 + early, tiles - 2 - early, small, begun)
+    *begun, one, two, mixer = own(True, 0, 2, scalars, ())
+    rows_one = swapped(one, "areal", 0)
+    rows_two = swapped(two, "areal", 1)
+    mob, acc, mob_sum, acc_sum = own(False, 1, tiles - 2, (*scalars[:3], mixer), begun)
 
     packet = pl.pallas_call(
         pack_columns,
@@ -519,7 +521,7 @@
         out_shape=jax.ShapeDtypeStruct((rows + ROWS, FIELDS * 32), f32),
         compiler_params=params(24),
         name="pack_columns",
-    )(above, below, mob, mob_sum, pressure, trans_x, trans_y, trans_z, pore_volume, acc_sum)
+    )(rows_one, rows_two, mob, mob_sum, pressure, trans_x, trans_y, trans_z, pore_volume, acc_sum)
 
     def residual(start, count, before):
         cells = rows * count * width
@@ -537,13 +539,11 @@
                 flops=150 * cells, transcendentals=0, bytes_accessed=4 * 31 * cells
             ),
             name="near_residual",
-        )(above, below, pressure, trans_x, trans_y, trans_z, mob, acc, *before)
-
-    left = moved(packet, "layer", 1)
-    near = residual(0, depth // 2, ())
-    packet, near = lax.optimization_barrier((packet, near))
-    right = moved(packet, "layer", -1)
-    near = residual(depth // 2, depth - depth // 2, (near,))
+        )(rows_one, rows_two, pressure, trans_x, trans_y, trans_z, mob, acc, *before)
+
+    columns_one = swapped(packet, "layer", 0)
+    columns_two = swapped(packet, "layer", 1)
+    near = residual(0, depth, ())
     planes = pl.BlockSpec((COMPS, 2, rows, width), lambda s: (0, s, 0, 0))
 
     extended = pltpu.VMEM((depth, rows + ROWS, width + LANES), f32)
@@ -565,7 +565,7 @@
         compiler_params=params(28),
         name="finish",
     )(
-        left, right, above, below,
+        columns_one, columns_two, rows_one, rows_two,
         pressure, trans_x, trans_y, trans_z, pore_volume, mob_sum, acc_sum, mob, near,
     )
 

time: 38.9 us -> 31 us (0.80)
  the two profiles are of different devices: /device:TPU:12 before, /device:TPU:5 now
where the time goes in v4:
time: 31 us; the launch traced here: 30.7 us
  Pallas kernels  17.9 us (58%)
  starting transfers between devices  11.8 us (38%)
  between operations  0.87 us (3%)
    ppermute x4, starting transfers between devices, swapped(): return lax.ppermute(block, axis, pairs + [(j, i) for i, j in pairs])  11.8 us
    pallas_call x2, Pallas kernels, own(): pl.pallas_call(functools.partial(own_cells, edge, start), grid=(count, pa...  9.43 us
    pallas_call x1, Pallas kernels, on_device(): pl.pallas_call(finish, grid=(depth // 2,), in_specs=[vmem] * 12 + [planes...  4.69 us
    pallas_call x1, Pallas kernels, residual(): pl.pallas_call(functools.partial(near_residual, start, count), grid=(coun...  2.76 us
    pallas_call x1, Pallas kernels, on_device(): pl.pallas_call(pack_columns, in_specs=[vmem] * 10, out_specs=vmem, out_sh...  1.05 us
  transfers between devices with their start and end apart: 4, of which 0 were waited for; matrix products, arithmetic and copies ran while one was open for 0% of the time, Pallas kernels for 22%

profile of v4, /device:TPU:5, one launch (start us, length us, event | category | flops | bytes accessed | tf_op | source)
XLA Modules:
  0.0 30.7 jit_solution(9959909568171856577)
XLA Ops:
  0.6 0.0 copy-start
  0.6 0.0 copy-start.4
  0.7 0.0 copy-start.7
  0.7 0.0 copy-start.9
  0.7 0.0 copy-start.8
  0.7 0.0 copy-start.6
  0.7 0.0 copy-start.5
  0.7 5.6 %edge_cells.1 = (f32[9,8,32,256]{3,2,1,0:T(8,128)S(1)}, f32[9,8,32,256]{3,2,1,0:T(8,128)S(1)}, f32[8,32,256]{2,1,0:T(8,128)S(1)}, f32[8,32,256]{2,1,0:T(8,128)S(...) custom-call(s32[4,8]{1,0:T(4,128)} %flags.3, f32[9]{0:T(128)} %vol.3, ...), custom_call_target="tpu_custom_call" | custom-call | flops 29491200 | bytes 5111808 | tf_op jit(solution)/shard_map/edge_cells/pallas_call | solution.py:494
  6.3 0.7 %collective-permute-start = (f32[5,32,256]{2,1,0:T(8,128)S(1)}, f32[5,32,256]{2,1,0:T(8,128)S(1)}, u32[]{:S(2)}, u32[]{:S(2)}) collective-permute-start(f32[5,32,256]{2,1,0:T(8,128)S(1)} %get-tuple-element.13), channel_id=1, source_target_pairs={{0,4},{8,12},{16,20},{24,28},{4,0},{12,8},{20,16},{28,24},{1,5},{9... | collective-permute-start | bytes 491528 | tf_op jit(solution)/shard_map/ppermute | solution.py:472
  7.0 4.5 %collective-permute-start.1 = (f32[5,32,256]{2,1,0:T(8,128)S(1)}, f32[5,32,256]{2,1,0:T(8,128)S(1)}, u32[]{:S(2)}, u32[]{:S(2)}) collective-permute-start(f32[5,32,256]{2,1,0:T(8,128)S(1)} %get-tuple-element.14), channel_id=1, source_target_pairs={{4,8},{12,16},{20,24},{8,4},{16,12},{24,20},{5,9},{13,17},{21,25},... | collective-permute-start | bytes 491528 | tf_op jit(solution)/shard_map/ppermute | solution.py:472
  11.5 0.0 copy-done
  11.6 0.0 copy-done.4
  11.6 0.0 copy-done.7
  11.6 0.0 copy-done.9
  11.6 0.0 copy-done.8
  11.6 0.0 copy-done.6
  11.6 0.0 copy-done.5
  11.6 0.0 copy-start.1
  11.6 0.0 copy-start.2
  11.6 0.0 copy-start.3
  11.6 3.8 %inner_cells.1 = (f32[9,8,32,256]{3,2,1,0:T(8,128)S(1)}, f32[9,8,32,256]{3,2,1,0:T(8,128)S(1)}, f32[8,32,256]{2,1,0:T(8,128)S(1)}, f32[8,32,256]{2,1,0:T(8,128)S(1)}) custom-call(s32[4,8]{1,0:T(4,128)S(1)} %copy-done.7, f32[9]{0:T(128)S(1)} %copy-done.8, f32[9]{0:T(128)S(1)} %copy-done.9, ...), custom_call_target="tpu_custom_call", output_to_operand_aliasing={{0}: (8, {}), {1}: (9, {}), {2}: (10, {}), {3}: (11, {})} | custom-call | flops 29491200 | bytes 5111808 | tf_op jit(solution)/shard_map/inner_cells/pallas_call | solution.py:494
  15.5 0.0 collective-permute-done.rows_one
  15.5 0.0 collective-permute-done.1.rows_two
  15.5 0.0 copy-done.1
  15.5 0.0 copy-done.2
  15.5 1.1 %pack_columns.1 = f32[40,512]{1,0:T(8,128)S(1)} custom-call(f32[5,32,256]{2,1,0:T(8,128)S(1)} %collective-permute-done.rows_one, f32[5,32,256]{2,1,0:T(8,128)S(1)} %collective-permute-done.1.rows_two, f32[9,8,32,256]{3,2,1,0:T(8,128)S(1)} %get-tuple-element.20.mob, f32[8,32,256]{2,1,0:T(8,128)S(1)} %get-tuple-element.21.mob_sum, f32[8,32,256]{2,1,0:T(8,128)S(1)} %copy-done, ...), custom_call_target="tpu_custom_call" | custom-call | tf_op jit(solution)/shard_map/pack_columns/pallas_call | solution.py:517
  16.6 0.7 %collective-permute-start.3 = (f32[40,512]{1,0:T(8,128)S(1)}, f32[40,512]{1,0:T(8,128)S(1)}, u32[]{:S(2)}, u32[]{:S(2)}) collective-permute-start(f32[40,512]{1,0:T(8,128)S(1)} %pack_columns.1), channel_id=1, source_target_pairs={{1,2},{2,1},{5,6},{6,5},{9,10},{10,9},{13,14},{14,13},{17,18},{18,... | collective-permute-start | bytes 245768 | tf_op jit(solution)/shard_map/ppermute | solution.py:472
  17.3 5.9 %collective-permute-start.2 = (f32[40,512]{1,0:T(8,128)S(1)}, f32[40,512]{1,0:T(8,128)S(1)}, u32[]{:S(2)}, u32[]{:S(2)}) collective-permute-start(f32[40,512]{1,0:T(8,128)S(1)} %pack_columns.1), channel_id=1, source_target_pairs={{0,1},{2,3},{1,0},{3,2},{4,5},{6,7},{5,4},{7,6},{8,9},{10,11},{9,8... | collective-permute-start | bytes 245768 | tf_op jit(solution)/shard_map/ppermute | solution.py:472
  23.2 2.8 %near_residual.1.near = f32[9,8,32,256]{3,2,1,0:T(8,128)S(1)} custom-call(f32[5,32,256]{2,1,0:T(8,128)S(1)} %collective-permute-done.rows_one, f32[5,32,256]{2,1,0:T(8,128)S(1)} %collective-permute-done.1.rows_two, f32[8,32,256]{2,1,0:T(8,128)S(1)} %copy-done, f32[8,32,256]{2,1,0:T(8,128)S(1)} %copy-done.1, f32[8,32,256]{2,1,0:T(8,128)S(1)} %copy-done.2, ...), custom_call_target="tpu_custom_call" | custom-call | flops 9830400 | bytes 8126464 | tf_op jit(solution)/shard_map/near_residual/pallas_call | solution.py:529
  26.0 0.0 collective-permute-done.3.columns_two
  26.0 0.0 collective-permute-done.2.columns_one
  26.0 4.7 %finish.1 = (f32[9,8,32,256]{3,2,1,0:T(8,128)}, f32[8,32,256]{2,1,0:T(8,128)}) custom-call(f32[40,512]{1,0:T(8,128)S(1)} %collective-permute-done.2.columns_one, f32[40,512]{1,0:T(8,128)S(1)} %collective-permute-done.3.columns_two, f32[5,32,256]{2,1,0:T(8,128)S(1)} %collective-permute-done.rows_one, f32[5,32,256]{2,1,0:T(8,128)S(1)} %collective-permute-done.1.rows_two, ...), custom_call_target="tpu_custom_call" | custom-call | tf_op jit(solution)/shard_map/finish/pallas_call | solution.py:551
  (1 shorter events, 0.0 us)
Async XLA Ops:
  0.6 10.9 %copy-start = (f32[8,32,256]{2,1,0:T(8,128)S(1)}, f32[8,32,256]{2,1,0:T(8,128)}, u32[]{:S(2)}) copy-start(f32[8,32,256]{2,1,0:T(8,128)} %press.9) | copy-start | bytes 786436
  0.6 10.9 %copy-start.4 = (f32[8,32,256]{2,1,0:T(8,128)S(1)}, f32[8,32,256]{2,1,0:T(8,128)}, u32[]{:S(2)}) copy-start(f32[8,32,256]{2,1,0:T(8,128)} %pore.7) | copy-start | bytes 786436
  0.7 10.9 %copy-start.7 = (s32[4,8]{1,0:T(4,128)S(1)}, s32[4,8]{1,0:T(4,128)}, u32[]{:S(2)}) copy-start(s32[4,8]{1,0:T(4,128)} %flags.3) | copy-start | bytes 388
  0.7 10.9 %copy-start.9 = (f32[9]{0:T(128)S(1)}, f32[9]{0:T(128)}, u32[]{:S(2)}) copy-start(f32[9]{0:T(128)} %slope.3) | copy-start | bytes 112
  0.7 10.9 %copy-start.8 = (f32[9]{0:T(128)S(1)}, f32[9]{0:T(128)}, u32[]{:S(2)}) copy-start(f32[9]{0:T(128)} %vol.3) | copy-start | bytes 112
  0.7 10.9 %copy-start.6 = (f32[9,8,32,256]{3,2,1,0:T(8,128)S(1)}, f32[9,8,32,256]{3,2,1,0:T(8,128)}, u32[]{:S(2)}) copy-start(f32[9,8,32,256]{3,2,1,0:T(8,128)} %mass.3) | copy-start | bytes 7077892
  0.7 10.9 %copy-start.5 = (f32[9,8,32,256]{3,2,1,0:T(8,128)S(1)}, f32[9,8,32,256]{3,2,1,0:T(8,128)}, u32[]{:S(2)}) copy-start(f32[9,8,32,256]{3,2,1,0:T(8,128)} %comp.3) | copy-start | bytes 7077892
  6.3 9.2 %collective-permute-start = (f32[5,32,256]{2,1,0:T(8,128)S(1)}, f32[5,32,256]{2,1,0:T(8,128)S(1)}, u32[]{:S(2)}, u32[]{:S(2)}) collective-permute-start(f32[5,32,256]{2,1,0:T(8,128)S(1)} %get-tuple-element.13), channel_id=1, source_target_pairs={{0,4},{8,12},{16,20},{24,28},{4,0},{12,8},{20,16},{28,24},{1,5},{9... | collective-permute-start | bytes 491528 | tf_op jit(solution)/shard_map/ppermute | solution.py:472
  7.0 8.5 %collective-permute-start.1 = (f32[5,32,256]{2,1,0:T(8,128)S(1)}, f32[5,32,256]{2,1,0:T(8,128)S(1)}, u32[]{:S(2)}, u32[]{:S(2)}) collective-permute-start(f32[5,32,256]{2,1,0:T(8,128)S(1)} %get-tuple-element.14), channel_id=1, source_target_pairs={{4,8},{12,16},{20,24},{8,4},{16,12},{24,20},{5,9},{13,17},{21,25},... | collective-permute-start | bytes 491528 | tf_op jit(solution)/shard_map/ppermute | solution.py:472
  11.6 3.9 %copy-start.1 = (f32[8,32,256]{2,1,0:T(8,128)S(1)}, f32[8,32,256]{2,1,0:T(8,128)}, u32[]{:S(2)}) copy-start(f32[8,32,256]{2,1,0:T(8,128)} %tx.5) | copy-start | bytes 786436
  11.6 3.9 %copy-start.2 = (f32[8,32,256]{2,1,0:T(8,128)S(1)}, f32[8,32,256]{2,1,0:T(8,128)}, u32[]{:S(2)}) copy-start(f32[8,32,256]{2,1,0:T(8,128)} %ty.5) | copy-start | bytes 786436
  11.6 3.9 %copy-start.3 = (f32[8,32,256]{2,1,0:T(8,128)S(1)}, f32[8,32,256]{2,1,0:T(8,128)}, u32[]{:S(2)}) copy-start(f32[8,32,256]{2,1,0:T(8,128)} %tz.5) | copy-start | bytes 786436
  16.6 9.4 %collective-permute-start.3 = (f32[40,512]{1,0:T(8,128)S(1)}, f32[40,512]{1,0:T(8,128)S(1)}, u32[]{:S(2)}, u32[]{:S(2)}) collective-permute-start(f32[40,512]{1,0:T(8,128)S(1)} %pack_columns.1), channel_id=1, source_target_pairs={{1,2},{2,1},{5,6},{6,5},{9,10},{10,9},{13,14},{14,13},{17,18},{18,... | collective-permute-start | bytes 245768 | tf_op jit(solution)/shard_map/ppermute | solution.py:472
  17.3 8.7 %collective-permute-start.2 = (f32[40,512]{1,0:T(8,128)S(1)}, f32[40,512]{1,0:T(8,128)S(1)}, u32[]{:S(2)}, u32[]{:S(2)}) collective-permute-start(f32[40,512]{1,0:T(8,128)S(1)} %pack_columns.1), channel_id=1, source_target_pairs={{0,1},{2,3},{1,0},{3,2},{4,5},{6,7},{5,4},{7,6},{8,9},{10,11},{9,8... | collective-permute-start | bytes 245768 | tf_op jit(solution)/shard_map/ppermute | solution.py:472
